TPU v7x, 32 devices: a whole 2x2x4 slice. The times are simulated.
32 devices in a mesh: row: 8 (over y, x, core), col: 4 (over z).
Axes of the slice: x: 2, y: 2, z: 4, core: 2. Of those that a mesh axis runs over, the one named last changes fastest.
Arguments:
- panel_cols: float32 [256, 8192], P('col', 'row'), as said below
- window_cols: float32 [16384, 8192], P('col', 'row'), may hold values from -6 to 6
Outputs:
- triangle: float32 [256, 256], replicated
- top_rows: float32 [16384, 256], P(('col', 'row'))
- residual: float32 [16384, 8192], P('col', 'row')
Inputs may be any that keep to these rules, and one draw needn't show every extreme that they name: `panel_cols`: the 256 rows are linearly independent over the 1024 columns of every block of row.
All inputs are finite; a program needn't handle non-finite values.
Results may differ from a plain program's by a relative error of at most 0.000084.
Values sent between devices are 32-bit elements; how exact they have to be, the bound alone decides.
No kernel may reach another device: no remote copies, remote signals or barrier semaphores. Data moves between devices by JAX's collectives and lax.ppermute only.
A program may use at most 128 MiB of HBM per device.

v0:
```python
import functools

import jax
import jax.numpy as jnp
from jax import lax
from jax.experimental import pallas as pl
from jax.experimental.pallas import tpu as pltpu
from jax.sharding import PartitionSpec as P

precise = lax.Precision.HIGHEST
f32, bf16 = jnp.float32, jnp.bfloat16
BLOCK = 32
MIB = 1 << 20
ROOM = 24 * MIB
LONG = pl.CostEstimate(flops=100_000_000_000, bytes_accessed=1, transcendentals=0)
BRIEF = pl.CostEstimate(flops=1, bytes_accessed=1, transcendentals=0)


def dot(left, right, dims, precision=None):
    return lax.dot_general(
        left, right, (dims, ((), ())), precision=precision, preferred_element_type=f32
    )


def split(value):
    high = value.astype(bf16)
    return high, (value - high.astype(f32)).astype(bf16)


def after(value, *others):
    return lax.optimization_barrier((value, *others))[0]


def gram_kernel(place_ref, *refs):
    shards, (whole_ref, high_ref, low_ref, gram_ref) = refs[:-4], refs[-4:]
    rows = shards[0].shape[0]
    for step, shard in enumerate(shards):
        owner = lax.rem(place_ref[0] + step, len(shards))
        whole_ref[pl.ds(pl.multiple_of(owner * rows, rows), rows), :] = shard[...]
    whole = whole_ref[...]
    gram_ref[...] = dot(whole, whole, ((1,), (1,)), precise)
    high_ref[...], low_ref[...] = split(whole)


def gram_call(place, shards):
    rows, columns = shards[0].shape
    panel = rows * len(shards)
    in_vmem = pl.BlockSpec(memory_space=pltpu.VMEM)
    return pl.pallas_call(
        gram_kernel,
        in_specs=[pl.BlockSpec(memory_space=pltpu.SMEM)] + [in_vmem] * len(shards),
        out_specs=[in_vmem] * 4,
        out_shape=[
            jax.ShapeDtypeStruct((panel, columns), f32),
            jax.ShapeDtypeStruct((panel, columns), bf16),
            jax.ShapeDtypeStruct((panel, columns), bf16),
            jax.ShapeDtypeStruct((panel, panel), f32),
        ],
        compiler_params=pltpu.CompilerParams(vmem_limit_bytes=24 * MIB),
        cost_estimate=LONG,
        name="gram",
    )(place, *shards)


def hold_kernel(table_ref, place_ref, window_ref, high_ref, low_ref, held, arrivals):
    slots, rows, _ = held.shape
    count = window_ref.shape[0] // rows

    def arriving(step):
        start = pl.multiple_of(step * rows, rows)
        slot = lax.rem(step, slots)
        return pltpu.make_async_copy(
            window_ref.at[pl.ds(start, rows), :], held.at[slot], arrivals.at[slot]
        )

    for step in range(min(slots, count)):
        arriving(step).start()

    @pl.loop(0, count)
    def _(step):
        arriving(step).wait()
        high, low = split(held[lax.rem(step, slots)])
        here = pl.ds(pl.multiple_of(step * rows, rows), rows)
        high_ref[here, :] = high
        low_ref[here, :] = low

        @pl.when(step + slots < count)
        def _():
            arriving(step + slots).start()


def hold_call(table, place, window):
    rows, columns = window.shape
    tile = min(256, rows)
    scalars = pl.BlockSpec(memory_space=pltpu.SMEM)
    return pl.pallas_call(
        hold_kernel,
        in_specs=[scalars, scalars, pl.BlockSpec(memory_space=pl.ANY)],
        out_specs=[pl.BlockSpec(memory_space=pltpu.VMEM)] * 2,
        scratch_shapes=[
            pltpu.VMEM((4, tile, columns), f32),
            pltpu.SemaphoreType.DMA((4,)),
        ],
        out_shape=[jax.ShapeDtypeStruct(window.shape, bf16)] * 2,
        compiler_params=pltpu.CompilerParams(vmem_limit_bytes=ROOM),
        cost_estimate=BRIEF,
        name="hold",
    )(table, place, window)


def cross_kernel(first, each, table_ref, window_high, window_low, high_ref, low_ref, *outs):
    tile = outs[0].shape[0] // each
    dims = ((1,), (1,))
    pair = 3 - len(outs) if each % 2 == 0 else 1

    @pl.loop(0, each // pair)
    def _(step):
        entries = [first + step * pair + place for place in range(pair)]
        rows = [pl.ds(pl.multiple_of(table_ref[at], tile), len(outs) * tile) for at in entries]
        window = [
            jnp.concatenate([term[at, :] for at in rows], 0) for term in (window_high, window_low)
        ]
        result = dot(window[0], high_ref[...], dims) + (
            dot(window[0], low_ref[...], dims) + dot(window[1], high_ref[...], dims)
        )
        here = pl.ds(pl.multiple_of(step * pair * tile, tile), pair * tile)
        for part, cross_ref in enumerate(outs):
            cross_ref[here, :] = result[part * pair * tile : (part + 1) * pair * tile]


def cross_call(table, first, parts, each, tile, window, panel, cost):
    in_vmem = pl.BlockSpec(memory_space=pltpu.VMEM)
    return pl.pallas_call(
        functools.partial(cross_kernel, first, each),
        in_specs=[pl.BlockSpec(memory_space=pltpu.SMEM)] + [in_vmem] * 4,
        out_specs=[in_vmem] * parts,
        out_shape=[jax.ShapeDtypeStruct((each * tile, panel[0].shape[0]), f32)] * parts,
        compiler_params=pltpu.CompilerParams(vmem_limit_bytes=ROOM),
        cost_estimate=cost,
        name="cross",
    )(table, *window, *panel)


def residual_kernel(firsts, each, table_ref, window_high, window_low, weight_ref, *refs):
    totals, (out_ref, sent, departures) = refs[: len(firsts)], refs[-3:]
    _, tile, columns = sent.shape
    chunk = min(256, columns)

    def leaving(place, entry, part):
        rows = pl.ds(pl.multiple_of(table_ref[entry], tile), tile)
        here = pl.ds(part * chunk, chunk)
        return pltpu.make_async_copy(
            sent.at[place, :, here], out_ref.at[rows, here], departures.at[place, part]
        )

    for part, (first, total) in enumerate(zip(firsts, totals)):
        high, low = split(total[...])
        terms = jnp.concatenate([high, high, low], 1)
        rows = [pl.ds(pl.multiple_of(table_ref[first + at], tile), tile) for at in range(each)]
        for start in range(0, columns, chunk):
            here = slice(start, start + chunk)
            product = dot(terms, weight_ref[:, here], ((1,), (0,)))
            for at in range(each):
                window = window_high[rows[at], here].astype(f32)
                window = window + window_low[rows[at], here].astype(f32)
                sent[part * each + at, :, here] = window - product[at * tile : (at + 1) * tile]
                leaving(part * each + at, first + at, start // chunk).start()

    for part, first in enumerate(firsts):
        for at in range(each):
            for piece in range(columns // chunk):
                leaving(part * each + at, first + at, piece).wait()


def residual_call(table, firsts, tile, window, weight, totals, before, cost=BRIEF):
    (rows, columns), each = window[0].shape, totals[0].shape[0] // tile
    in_vmem = pl.BlockSpec(memory_space=pltpu.VMEM)
    operands = [table, *window, weight, *totals]
    in_specs = [pl.BlockSpec(memory_space=pltpu.SMEM)] + [in_vmem] * (len(operands) - 1)
    aliases = {}
    if before is not None:
        aliases = {len(operands): 0}
        operands.append(before)
        in_specs.append(pl.BlockSpec(memory_space=pl.ANY))
    return pl.pallas_call(
        functools.partial(residual_kernel, firsts, each),
        in_specs=in_specs,
        out_specs=pl.BlockSpec(memory_space=pl.ANY),
        scratch_shapes=[
            pltpu.VMEM((len(firsts) * each, tile, columns), f32),
            pltpu.SemaphoreType.DMA((len(firsts) * each, columns // min(256, columns))),
        ],
        out_shape=jax.ShapeDtypeStruct((rows, columns), f32),
        input_output_aliases=aliases,
        compiler_params=pltpu.CompilerParams(vmem_limit_bytes=ROOM),
        cost_estimate=cost,
        name="residual",
    )(*operands)


def eliminate(diagonal):
    size, lanes, tile = BLOCK, 128, 8
    tiles = size // tile
    row_at = [lax.broadcasted_iota(jnp.int32, (tile, lanes), 0) + tile * t for t in range(tiles)]
    lane_at = lax.broadcasted_iota(jnp.int32, (tile, lanes), 1)
    spread = [
        [
            jnp.broadcast_to(diagonal[tile * t : tile * (t + 1), k : k + 1], (tile, lanes))
            for t in range(tiles)
        ]
        for k in range(size)
    ]
    inverse = [jnp.where(row_at[t] == lane_at, 1.0, 0.0) for t in range(tiles)]
    lower = [jnp.zeros((tile, lanes), f32) for _ in range(tiles)]
    scale = [jnp.zeros((tile, lanes), f32) for _ in range(tiles)]
    for j in range(size):
        own, at = j // tile, j % tile
        pivot = spread[j][own][at : at + 1, :]
        reciprocal = 1.0 / pivot
        root = lax.rsqrt(pivot)
        inverse_row = inverse[own][at : at + 1, :]
        factor = {}
        for t in range(own, tiles):
            column = spread[j][t]
            factor[t] = column * reciprocal
            if t == own:
                factor[t] = jnp.where(row_at[t] > j, factor[t], 0.0)
                scale[t] = jnp.where(row_at[t] == j, root, scale[t])
                lower[t] = jnp.where((lane_at == j) & (row_at[t] >= j), column * root, lower[t])
            else:
                lower[t] = jnp.where(lane_at == j, column * root, lower[t])
            inverse[t] = inverse[t] - factor[t] * inverse_row
        for k in range(j + 1, size):
            entry = spread[j][k // tile][k % tile : k % tile + 1, :]
            for t in range(k // tile, tiles):
                spread[k][t] = spread[k][t] - factor[t] * entry
    inverse = [inverse[t] * scale[t] for t in range(tiles)]
    return jnp.concatenate(lower, 0), jnp.concatenate(inverse, 0)


def factor_kernel(begin, end, last, ins, outs):
    state_ref, lower_ref = outs[:2]
    state_ref[...] = ins[0][...]
    if begin:
        lower_ref[...] = ins[1][...]
    size = state_ref.shape[0]
    column_at = lax.broadcasted_iota(jnp.int32, (BLOCK, size), 1)
    row_at = lax.broadcasted_iota(jnp.int32, (BLOCK, size), 0)
    for step in range(begin, end):
        start, stop = step * BLOCK, (step + 1) * BLOCK
        rows = state_ref[start:stop, :]
        lower, inverse = eliminate(rows[:, start:stop])
        lower_ref[start:stop, :] = lower
        inside = (column_at >= start) & (column_at < stop)
        rows = jnp.where(inside, jnp.where(column_at - start == row_at, 1.0, 0.0), rows)
        done = dot(inverse[:, :BLOCK], rows, ((1,), (0,)), precise)
        state_ref[start:stop, :] = done
        if stop < size:
            upper = jnp.where(column_at >= stop, done, 0.0)
            update = dot(upper, done, ((0,), (0,)), precise)[stop:, :]
            below_at = lax.broadcasted_iota(jnp.int32, (size - stop, size), 1)
            below = jnp.where(
                (below_at >= start) & (below_at < stop), 0.0, state_ref[stop:, :]
            )
            state_ref[stop:, :] = below - update
    if last:
        whole_ref = ins[2]
        triangle_ref, inverse_ref, weight_ref = outs[2:]
        column_at = lax.broadcasted_iota(jnp.int32, (size, size), 1)
        row_at = lax.broadcasted_iota(jnp.int32, (size, size), 0)
        edge = (row_at // BLOCK + 1) * BLOCK
        state = state_ref[...]
        inverse = jnp.where(column_at <= row_at, state, 0.0)
        lower = lower_ref[...]
        wide = jnp.concatenate([lower] * (size // lower.shape[1]), 1)
        for step in range(size // BLOCK):
            start, stop = step * BLOCK, (step + 1) * BLOCK
            shift = start % lower.shape[1]
            part = wide[start:stop, :]
            if shift:
                part = pltpu.roll(part, shift, 1)
            lower_full = jnp.where(
                (column_at[start:stop, :] >= start) & (column_at[start:stop, :] < stop), part, 0.0
            )
            state_ref[start:stop, :] = lower_full
        triangle_ref[...] = jnp.where(column_at >= edge, state, 0.0) + state_ref[...].T
        half = dot(inverse, whole_ref[...], ((1,), (0,)), precise)
        inverse_ref[...] = inverse
        weight = dot(inverse, half, ((0,), (0,)), precise)
        high, low = split(weight)
        for term, part in enumerate((high, low, high)):
            weight_ref[term * size : (term + 1) * size, :] = part


def factor_call(begin, end, operands, whole=None):
    size = operands[0].shape[1]
    operands = list(operands)
    shapes = [
        jax.ShapeDtypeStruct((size, size), f32),
        jax.ShapeDtypeStruct((size, 128), f32),
    ]
    if whole is not None:
        operands.append(whole)
        shapes += [
            jax.ShapeDtypeStruct((size, size), f32),
            jax.ShapeDtypeStruct((size, size), f32),
            jax.ShapeDtypeStruct((3 * size, whole.shape[1]), bf16),
        ]
    in_specs = [pl.BlockSpec(memory_space=pltpu.VMEM)] * len(operands)

    def body(*refs):
        factor_kernel(begin, end, whole is not None, refs[: len(operands)], refs[len(operands) :])

    return pl.pallas_call(
        body,
        out_shape=shapes,
        in_specs=in_specs,
        out_specs=[pl.BlockSpec(memory_space=pltpu.VMEM)] * len(shapes),
        compiler_params=pltpu.CompilerParams(vmem_limit_bytes=24 * MIB),
        cost_estimate=BRIEF,
        name="factor",
    )(*operands)


def flip(value, bit, size):
    return lax.ppermute(value, "row", [(i, i ^ bit) for i in range(size)])


def exchange(value, step, bits):
    size = 2 << len(bits)
    return lax.ppermute(
        value, "row", [(i, i ^ (bits[-1 - step] if i & 1 else bits[step])) for i in range(size)]
    )


def relative_owners(bits):
    owners = [0]
    for bit in reversed(bits):
        owners = [owner | bit for owner in owners] + owners
    return owners


def sum_shares(kept, arrived, bits):
    pairs, count = [(kept, 0), (arrived, 0)], kept.shape[0]
    cut = lambda array, at: lax.slice_in_dim(array, at, at + count, axis=0)
    for step in range(len(bits)):
        count //= 2
        out, others = yield sum(cut(array, at) for array, at in pairs)
        pairs = [(array, at + count) for array, at in pairs]
        if others:
            pairs[0] = (after(pairs[0][0], *others), pairs[0][1])
        pairs.append((exchange(out, step, bits), 0))
    yield sum(cut(array, at) for array, at in pairs)


def gather_panel(shard, depth):
    up = [(i, (i - 1) % depth) for i in range(depth)]
    down = [(i, (i + 1) % depth) for i in range(depth)]
    above = [lax.ppermute(shard, "col", up)]
    below = []
    later, _ = lax.optimization_barrier((shard, above[0]))
    for step in range(2, depth):
        if step % 2 == 0:
            above.append(lax.ppermute(above[-1], "col", up))
        else:
            below.append(lax.ppermute(below[-1] if below else later, "col", down))
    return [shard, *above, *below[::-1]]


def spread(part, bits, *others):
    for step in reversed(range(1, len(bits))):
        part = jnp.concatenate([after(exchange(part, step, bits), *others), part], 0)
    return part


def local(panel_cols, window_cols):
    size = lax.axis_size("row")
    depth = lax.axis_size("col")
    here = lax.axis_index("row").astype(jnp.int32)
    place = lax.axis_index("col").astype(jnp.int32).reshape(1)
    bits = [1 << shift for shift in range(1, size.bit_length() - 1)]
    steps = len(bits)
    share = window_cols.shape[0] // size

    tile = share // 2

    owners = [jnp.asarray(relative_owners(order), jnp.int32) for order in (bits, bits[::-1])]
    table_of = lambda device: share * (device ^ jnp.where(device & 1, owners[1], owners[0]))
    kept, given = table_of(here), table_of(here ^ 1)
    count = kept.shape[0]
    table = jnp.concatenate([kept, kept + tile, given, given + tile])
    entry = lambda side, half: (side * 2 + half) * count

    shards = gather_panel(panel_cols, depth)
    window = hold_call(table, place, window_cols)
    whole, high, low, gram = gram_call(after(place, window[0]), shards)

    def products(side, half, parts, cost, *others):
        first = after(table, *others)
        return cross_call(first, entry(side, half), parts, count, tile, window, (high, low), cost)

    (given,) = products(1, 0, 1, BRIEF, gram)
    arrived = flip(given, 1, size)
    gram = gram + exchange(gram, 0, bits)
    (kept,) = products(0, 0, 1, LONG, given)
    early = sum_shares(kept, arrived, bits)
    early_sum = next(early)
    gram = after(gram, kept)
    (given,) = products(1, 1, 1, BRIEF, early_sum, gram)
    arrived = flip(given, 1, size)
    for step in range(1, steps):
        gram = gram + after(exchange(gram, step, bits), given)
    (kept,) = products(0, 1, 1, LONG, given)
    late = sum_shares(after(kept, gram), arrived, bits)
    late_sum = next(late)
    gram = gram + flip(gram, 1, size)

    blocks = whole.shape[0] // BLOCK
    cuts = (0, blocks * 3 // 8, blocks * 6 // 8, blocks)
    state = factor_call(0, cuts[1], [after(gram, late_sum)])
    early_sum = early.send((early_sum, (state[0],)))
    late_sum = late.send((late_sum, (early_sum,)))
    state = factor_call(cuts[1], cuts[2], [after(state[0], early_sum, late_sum), state[1]])
    for _ in range(1, steps):
        early_sum = early.send((early_sum, (state[0],)))
    for _ in range(1, steps):
        late_sum = late.send((late_sum, (early_sum,)))
    _, _, triangle, inverse, weight = factor_call(
        cuts[2], blocks, [after(state[0], early_sum, late_sum), state[1]], whole
    )

    early_near = spread(early_sum, bits, weight)
    late_near = spread(late_sum, bits, early_near)
    early_far, late_far = [exchange(part, 0, bits) for part in (early_near, late_near)]
    nearer = lambda side, half: entry(side, half) + count // 2
    subtract = lambda firsts, *others: residual_call(table, firsts, tile, window, weight, *others)
    parts = [early_near, flip(early_near, 1, size), late_near]
    residual = subtract([nearer(0, 0), nearer(1, 0), nearer(0, 1)], parts, None)
    late_back = flip(late_near, 1, size)
    early_far, residual = lax.optimization_barrier((early_far, residual))
    residual = subtract([nearer(1, 1), entry(0, 0)], [late_back, early_far], residual)
    late_far, residual = lax.optimization_barrier((late_far, residual))
    parts = [flip(early_far, 1, size), late_far, flip(late_far, 1, size)]
    residual = subtract([entry(1, 0), entry(0, 1), entry(1, 1)], parts, residual)
    summed = jnp.concatenate([after(early_sum, late_far), late_sum], 0)
    top_rows = dot(summed, inverse, ((1,), (1,)), precise)
    return triangle, top_rows, residual


def solution(mesh):
    return jax.shard_map(
        local,
        mesh=mesh,
        in_specs=(P("col", "row"), P("col", "row")),
        out_specs=(P(), P(("col", "row"), None), P("col", "row")),
        check_vma=False,
    )
```

profile of v0, /device:TPU:0, one launch (start us, length us, event | category | flops | bytes accessed | tf_op | source)
XLA Modules:
  0.0 85.6 jit_solution(5280606329353878852)
XLA Ops:
  0.6 5.1 %collective-permute-start = (f32[64,1024]{1,0:T(8,128)}, f32[64,1024]{1,0:T(8,128)S(1)}, u32[]{:S(2)}, u32[]{:S(2)}) collective-permute-start(f32[64,1024]{1,0:T(8,128)} %refs_0_.1), channel_id=1, source_target_pairs={{0,3},{1,0},{2,1},{3,2},{4,7},{5,4},{6,5},{7,6},{8,11},{9,8},{10,9... | collective-permute-start | bytes 786440 | tf_op jit(solution)/shard_map/ppermute | solution.py:359
  5.7 6.1 %collective-permute-done.refs_1_ = f32[64,1024]{1,0:T(8,128)S(1)} collective-permute-done((f32[64,1024]{1,0:T(8,128)}, f32[64,1024]{1,0:T(8,128)S(1)}, u32[]{:S(2)}, u32[]{:S(2)}) %collective-permute-start) | collective-permute-done | bytes 262176 | tf_op jit(solution)/shard_map/ppermute | solution.py:359
  12.0 4.0 %collective-permute-start.1 = (f32[64,1024]{1,0:T(8,128)S(1)}, f32[64,1024]{1,0:T(8,128)S(1)}, u32[]{:S(2)}, u32[]{:S(2)}) collective-permute-start(f32[64,1024]{1,0:T(8,128)S(1)} %collective-permute-done.refs_1_), channel_id=1, source_target_pairs={{0,3},{1,0},{2,1},{3,2},{4,7},{5,4},{6,5},{7,6},{8,11},{9,8},{10,9... | collective-permute-start | bytes 786440 | tf_op jit(solution)/shard_map/ppermute | solution.py:364
  16.0 0.7 broadcast_add_fusion.1
  16.7 7.4 %hold.1 = (bf16[4096,1024]{1,0:T(8,128)(2,1)S(1)}, bf16[4096,1024]{1,0:T(8,128)(2,1)S(1)}) custom-call(s32[16]{0:T(128)S(1)} %pad_add_fusion.table_ref, s32[1]{0:T(128)} %bitcast.place_ref, f32[4096,1024]{1,0:T(8,128)} %window_ref.1), custom_call_target="tpu_custom_call" | custom-call | flops 1 | bytes 1 | tf_op jit(solution)/shard_map/hold/pallas_call | solution.py:96
  24.5 1.3 %gram.1 = (f32[256,1024]{1,0:T(8,128)S(1)}, bf16[256,1024]{1,0:T(8,128)(2,1)S(1)}, bf16[256,1024]{1,0:T(8,128)(2,1)S(1)}, f32[256,256]{1,0:T(8,128)S(1)}) custom-call(s32[1]{0:T(128)} %bitcast.place_ref, f32[64,1024]{1,0:T(8,128)S(1)} %copy-done, f32[64,1024]{1,0:T(8,128)S(1)} %collective-permute-done.refs_1_, ...), custom_call_target="tpu_custom_call" | custom-call | flops 99999997952 | bytes 1 | tf_op jit(solution)/shard_map/gram/pallas_call | solution.py:49
  25.7 1.6 %collective-permute-start.3 = (f32[256,256]{1,0:T(8,128)S(1)}, f32[256,256]{1,0:T(8,128)S(1)}, u32[]{:S(2)}, u32[]{:S(2)}) collective-permute-start(f32[256,256]{1,0:T(8,128)S(1)} %get-tuple-element.42), channel_id=1, source_target_pairs={{0,8},{4,20},{8,0},{12,28},{16,24},{20,4},{24,16},{28,12},{1,9},{5... | collective-permute-start | bytes 786440 | tf_op jit(solution)/shard_map/ppermute | solution.py:331
  27.3 2.6 %cross.4 = f32[1024,256]{1,0:T(8,128)S(1)} custom-call(s32[16]{0:T(128)S(1)} %pad_add_fusion.table_ref, bf16[4096,1024]{1,0:T(8,128)(2,1)S(1)} %get-tuple-element.39.window_high, bf16[4096,1024]{1,0:T(8,128)(2,1)S(1)} %get-tuple-element.44.window_low, bf16[256,1024]{1,0:T(8,128)(2,1)S(1)} %get-tuple-element.45.high_ref, ...), custom_call_target="tpu_custom_call" | custom-call | flops 1 | bytes 1 | tf_op jit(solution)/shard_map/cross/pallas_call | solution.py:133
  30.0 2.6 %cross.5 = f32[1024,256]{1,0:T(8,128)S(1)} custom-call(s32[16]{0:T(128)S(1)} %pad_add_fusion.table_ref, bf16[4096,1024]{1,0:T(8,128)(2,1)S(1)} %get-tuple-element.39.window_high, bf16[4096,1024]{1,0:T(8,128)(2,1)S(1)} %get-tuple-element.44.window_low, bf16[256,1024]{1,0:T(8,128)(2,1)S(1)} %get-tuple-element.45.high_ref, ...), custom_call_target="tpu_custom_call" | custom-call | flops 99999997952 | bytes 1 | tf_op jit(solution)/shard_map/cross/pallas_call | solution.py:133
  32.6 1.6 %collective-permute-start.4 = (f32[256,256]{1,0:T(8,128)S(1)}, f32[256,256]{1,0:T(8,128)S(1)}, u32[]{:S(2)}, u32[]{:S(2)}) collective-permute-start(f32[256,256]{1,0:T(8,128)S(1)} %add.53), channel_id=1, source_target_pairs={{0,16},{4,12},{8,24},{12,4},{16,0},{20,28},{24,8},{28,20},{1,17},{... | collective-permute-start | bytes 786440 | tf_op jit(solution)/shard_map/ppermute | solution.py:331
  34.2 1.2 %collective-permute-start.8 = (f32[512,256]{1,0:T(8,128)S(1)}, f32[512,256]{1,0:T(8,128)S(1)}, u32[]{:S(2)}, u32[]{:S(2)}) collective-permute-start(f32[512,256]{1,0:T(8,128)S(1)} %slice_add_fusion.1), channel_id=1, source_target_pairs={{0,8},{4,20},{8,0},{12,28},{16,24},{20,4},{24,16},{28,12},{1,9},{5... | collective-permute-start | bytes 1572872 | tf_op jit(solution)/shard_map/ppermute | solution.py:331
  35.4 2.6 %cross.6 = f32[1024,256]{1,0:T(8,128)S(1)} custom-call(s32[16]{0:T(128)S(1)} %pad_add_fusion.table_ref, bf16[4096,1024]{1,0:T(8,128)(2,1)S(1)} %get-tuple-element.39.window_high, bf16[4096,1024]{1,0:T(8,128)(2,1)S(1)} %get-tuple-element.44.window_low, bf16[256,1024]{1,0:T(8,128)(2,1)S(1)} %get-tuple-element.45.high_ref, ...), custom_call_target="tpu_custom_call" | custom-call | flops 1 | bytes 1 | tf_op jit(solution)/shard_map/cross/pallas_call | solution.py:133
  38.1 2.7 %cross.7 = f32[1024,256]{1,0:T(8,128)S(1)} custom-call(s32[16]{0:T(128)S(1)} %pad_add_fusion.table_ref, bf16[4096,1024]{1,0:T(8,128)(2,1)S(1)} %get-tuple-element.39.window_high, bf16[4096,1024]{1,0:T(8,128)(2,1)S(1)} %get-tuple-element.44.window_low, bf16[256,1024]{1,0:T(8,128)(2,1)S(1)} %get-tuple-element.45.high_ref, ...), custom_call_target="tpu_custom_call" | custom-call | flops 99999997952 | bytes 1 | tf_op jit(solution)/shard_map/cross/pallas_call | solution.py:133
  40.8 1.0 %collective-permute-done.4 = f32[256,256]{1,0:T(8,128)S(1)} collective-permute-done((f32[256,256]{1,0:T(8,128)S(1)}, f32[256,256]{1,0:T(8,128)S(1)}, u32[]{:S(2)}, u32[]{:S(2)}) %collective-permute-start.4) | collective-permute-done | bytes 262176 | tf_op jit(solution)/shard_map/ppermute | solution.py:331
  41.9 0.9 %collective-permute-start.9 = (f32[512,256]{1,0:T(8,128)S(1)}, f32[512,256]{1,0:T(8,128)S(1)}, u32[]{:S(2)}, u32[]{:S(2)}) collective-permute-start(f32[512,256]{1,0:T(8,128)S(1)} %slice_add_fusion), channel_id=1, source_target_pairs={{0,8},{4,20},{8,0},{12,28},{16,24},{20,4},{24,16},{28,12},{1,9},{5... | collective-permute-start | bytes 1572872 | tf_op jit(solution)/shard_map/ppermute | solution.py:331
  42.9 1.5 %collective-permute-done.6 = f32[256,256]{1,0:T(8,128)S(1)} collective-permute-done((f32[256,256]{1,0:T(8,128)S(1)}, f32[256,256]{1,0:T(8,128)S(1)}, u32[]{:S(2)}, u32[]{:S(2)}) %collective-permute-start.6) | collective-permute-done | bytes 262176 | tf_op jit(solution)/shard_map/ppermute | solution.py:326
  44.4 3.9 %factor.3 = (f32[256,256]{1,0:T(8,128)S(1)}, f32[256,128]{1,0:T(8,128)S(1)}) custom-call(f32[256,256]{1,0:T(8,128)S(1)} %add.56.refs_0_), custom_call_target="tpu_custom_call" | custom-call | flops 1 | bytes 1 | tf_op jit(solution)/shard_map/factor/pallas_call | solution.py:314
  48.4 1.6 %collective-permute-start.10 = (f32[256,256]{1,0:T(8,128)S(1)}, f32[256,256]{1,0:T(8,128)S(1)}, u32[]{:S(2)}, u32[]{:S(2)}) collective-permute-start(f32[256,256]{1,0:T(8,128)S(1)} %slice_add_fusion.8), channel_id=1, source_target_pairs={{0,16},{4,12},{8,24},{12,4},{16,0},{20,28},{24,8},{28,20},{1,17},{... | collective-permute-start | bytes 786440 | tf_op jit(solution)/shard_map/ppermute | solution.py:331
  50.0 1.2 %collective-permute-done.9 = f32[512,256]{1,0:T(8,128)S(1)} collective-permute-done((f32[512,256]{1,0:T(8,128)S(1)}, f32[512,256]{1,0:T(8,128)S(1)}, u32[]{:S(2)}, u32[]{:S(2)}) %collective-permute-start.9) | collective-permute-done | bytes 524320 | tf_op jit(solution)/shard_map/ppermute | solution.py:331
  51.2 1.6 %collective-permute-start.11 = (f32[256,256]{1,0:T(8,128)S(1)}, f32[256,256]{1,0:T(8,128)S(1)}, u32[]{:S(2)}, u32[]{:S(2)}) collective-permute-start(f32[256,256]{1,0:T(8,128)S(1)} %slice_add_fusion.6), channel_id=1, source_target_pairs={{0,16},{4,12},{8,24},{12,4},{16,0},{20,28},{24,8},{28,20},{1,17},{... | collective-permute-start | bytes 786440 | tf_op jit(solution)/shard_map/ppermute | solution.py:331
  52.8 3.9 %factor.4 = (f32[256,256]{1,0:T(8,128)S(1)}, f32[256,128]{1,0:T(8,128)S(1)}) custom-call(f32[256,256]{1,0:T(8,128)S(1)} %get-tuple-element.57.refs_0_, f32[256,128]{1,0:T(8,128)S(1)} %get-tuple-element.58.refs_1_), custom_call_target="tpu_custom_call" | custom-call | flops 1 | bytes 1 | tf_op jit(solution)/shard_map/factor/pallas_call | solution.py:314
  57.8 1.6 %collective-permute-start.12 = (f32[256,256]{1,0:T(8,128)S(1)}, f32[256,256]{1,0:T(8,128)S(1)}, u32[]{:S(2)}, u32[]{:S(2)}) collective-permute-start(f32[256,256]{1,0:T(8,128)S(1)} %fusion.2), channel_id=1, source_target_pairs={{0,16},{4,12},{8,24},{12,4},{16,0},{20,28},{24,8},{28,20},{1,17},{... | collective-permute-start | bytes 786440 | tf_op jit(solution)/shard_map/ppermute | solution.py:331
  59.3 4.5 %factor.5 = (f32[256,256]{1,0:T(8,128)}, f32[256,128]{1,0:T(8,128)}, f32[256,256]{1,0:T(8,128)}, f32[256,256]{1,0:T(8,128)S(1)}, bf16[768,1024]{1,0:T(8,128)(2,1)S(1)}) custom-call(f32[256,256]{1,0:T(8,128)S(1)} %get-tuple-element.62.refs_0_, f32[256,128]{1,0:T(8,128)S(1)} %get-tuple-element.63.refs_1_, f32[256,1024]{1,0:T(8,128)S(1)} %get-tuple-element.64.refs_2_), custom_call_target="tpu_custom_call" | custom-call | flops 1 | bytes 1 | tf_op jit(solution)/shard_map/factor/pallas_call | solution.py:314
  64.0 1.2 %collective-permute-start.16 = (f32[512,256]{1,0:T(8,128)S(1)}, f32[512,256]{1,0:T(8,128)S(1)}, u32[]{:S(2)}, u32[]{:S(2)}) collective-permute-start(f32[512,256]{1,0:T(8,128)S(1)} %pad_maximum_fusion.3.refs_0_), channel_id=1, source_target_pairs={{0,8},{4,20},{8,0},{12,28},{16,24},{20,4},{24,16},{28,12},{1,9},{5... | collective-permute-start | bytes 1572872 | tf_op jit(solution)/shard_map/ppermute | solution.py:331
  65.2 0.9 %collective-permute-done.12 = f32[256,256]{1,0:T(8,128)S(1)} collective-permute-done((f32[256,256]{1,0:T(8,128)S(1)}, f32[256,256]{1,0:T(8,128)S(1)}, u32[]{:S(2)}, u32[]{:S(2)}) %collective-permute-start.12) | collective-permute-done | bytes 262176 | tf_op jit(solution)/shard_map/ppermute | solution.py:331
  66.2 0.9 %collective-permute-start.14 = (f32[512,256]{1,0:T(8,128)S(1)}, f32[512,256]{1,0:T(8,128)S(1)}, u32[]{:S(2)}, u32[]{:S(2)}) collective-permute-start(f32[512,256]{1,0:T(8,128)S(1)} %pad_maximum_fusion.1.refs_2_), channel_id=1, source_target_pairs={{0,8},{4,20},{8,0},{12,28},{16,24},{20,4},{24,16},{28,12},{1,9},{5... | collective-permute-start | bytes 1572872 | tf_op jit(solution)/shard_map/ppermute | solution.py:331
  67.1 4.9 %residual.3.refs_2_ = f32[4096,1024]{1,0:T(8,128)} custom-call(s32[16]{0:T(128)S(1)} %pad_add_fusion.table_ref, bf16[4096,1024]{1,0:T(8,128)(2,1)S(1)} %get-tuple-element.39.window_high, bf16[4096,1024]{1,0:T(8,128)(2,1)S(1)} %get-tuple-element.44.window_low, bf16[768,1024]{1,0:T(8,128)(2,1)S(1)} %get-tuple-element.66.weight_ref, ...), custom_call_target="tpu_custom_call" | custom-call | flops 1 | bytes 1 | tf_op jit(solution)/shard_map/residual/pallas_call | solution.py:185
  72.0 1.2 %collective-permute-done.16.refs_1_ = f32[512,256]{1,0:T(8,128)S(1)} collective-permute-done((f32[512,256]{1,0:T(8,128)S(1)}, f32[512,256]{1,0:T(8,128)S(1)}, u32[]{:S(2)}, u32[]{:S(2)}) %collective-permute-start.16) | collective-permute-done | bytes 524320 | tf_op jit(solution)/shard_map/ppermute | solution.py:331
  73.2 3.6 %residual.4.refs_3_ = f32[4096,1024]{1,0:T(8,128)} custom-call(s32[16]{0:T(128)S(1)} %pad_add_fusion.table_ref, bf16[4096,1024]{1,0:T(8,128)(2,1)S(1)} %get-tuple-element.39.window_high, bf16[4096,1024]{1,0:T(8,128)(2,1)S(1)} %get-tuple-element.44.window_low, bf16[768,1024]{1,0:T(8,128)(2,1)S(1)} %get-tuple-element.66.weight_ref, ...), custom_call_target="tpu_custom_call", output_to_operand_aliasing={{}: (6, {})} | custom-call | flops 1 | bytes 1 | tf_op jit(solution)/shard_map/residual/pallas_call | solution.py:185
  76.9 2.0 %collective-permute-done.14.refs_1_ = f32[512,256]{1,0:T(8,128)S(1)} collective-permute-done((f32[512,256]{1,0:T(8,128)S(1)}, f32[512,256]{1,0:T(8,128)S(1)}, u32[]{:S(2)}, u32[]{:S(2)}) %collective-permute-start.14) | collective-permute-done | bytes 524320 | tf_op jit(solution)/shard_map/ppermute | solution.py:331
  78.8 1.4 %fusion = f32[512,256]{1,0:T(8,128)} fusion(f32[256,256]{1,0:T(8,128)S(1)} %get-tuple-element.73, f32[256,256]{1,0:T(8,128)S(1)} %fusion.2, f32[256,256]{1,0:T(8,128)S(1)} %fusion.3), kind=kOutput, calls=%fused_computation.2 | convolution fusion | flops 402784256 | bytes 1310720 | tf_op jit(solution)/shard_map/dot_general | solution.py:20
  80.8 4.7 %residual.5 = f32[4096,1024]{1,0:T(8,128)} custom-call(s32[16]{0:T(128)S(1)} %pad_add_fusion.table_ref, bf16[4096,1024]{1,0:T(8,128)(2,1)S(1)} %get-tuple-element.39.window_high, bf16[4096,1024]{1,0:T(8,128)(2,1)S(1)} %get-tuple-element.44.window_low, bf16[768,1024]{1,0:T(8,128)(2,1)S(1)} %get-tuple-element.66.weight_ref, ...), custom_call_target="tpu_custom_call", output_to_operand_aliasing={{}: (7, {})} | custom-call | flops 1 | bytes 1 | tf_op jit(solution)/shard_map/residual/pallas_call | solution.py:185
  (36 shorter events, 2.8 us)
Async XLA Ops:
  0.6 23.9 %copy-start = (f32[64,1024]{1,0:T(8,128)S(1)}, f32[64,1024]{1,0:T(8,128)}, u32[]{:S(2)}) copy-start(f32[64,1024]{1,0:T(8,128)} %refs_0_.1) | copy-start | bytes 786436
  0.6 11.2 %collective-permute-start = (f32[64,1024]{1,0:T(8,128)}, f32[64,1024]{1,0:T(8,128)S(1)}, u32[]{:S(2)}, u32[]{:S(2)}) collective-permute-start(f32[64,1024]{1,0:T(8,128)} %refs_0_.1), channel_id=1, source_target_pairs={{0,3},{1,0},{2,1},{3,2},{4,7},{5,4},{6,5},{7,6},{8,11},{9,8},{10,9... | collective-permute-start | bytes 786440 | tf_op jit(solution)/shard_map/ppermute | solution.py:359
  11.8 12.4 %collective-permute-start.2 = (f32[64,1024]{1,0:T(8,128)}, f32[64,1024]{1,0:T(8,128)S(1)}, u32[]{:S(2)}, u32[]{:S(2)}) collective-permute-start(f32[64,1024]{1,0:T(8,128)} %refs_0_.1), channel_id=1, source_target_pairs={{0,1},{1,2},{2,3},{3,0},{4,5},{5,6},{6,7},{7,4},{8,9},{9,10},{10,1... | collective-permute-start | bytes 786440 | tf_op jit(solution)/shard_map/ppermute | solution.py:366
  12.0 12.5 %collective-permute-start.1 = (f32[64,1024]{1,0:T(8,128)S(1)}, f32[64,1024]{1,0:T(8,128)S(1)}, u32[]{:S(2)}, u32[]{:S(2)}) collective-permute-start(f32[64,1024]{1,0:T(8,128)S(1)} %collective-permute-done.refs_1_), channel_id=1, source_target_pairs={{0,3},{1,0},{2,1},{3,2},{4,7},{5,4},{6,5},{7,6},{8,11},{9,8},{10,9... | collective-permute-start | bytes 786440 | tf_op jit(solution)/shard_map/ppermute | solution.py:364
  25.7 6.8 %collective-permute-start.3 = (f32[256,256]{1,0:T(8,128)S(1)}, f32[256,256]{1,0:T(8,128)S(1)}, u32[]{:S(2)}, u32[]{:S(2)}) collective-permute-start(f32[256,256]{1,0:T(8,128)S(1)} %get-tuple-element.42), channel_id=1, source_target_pairs={{0,8},{4,20},{8,0},{12,28},{16,24},{20,4},{24,16},{28,12},{1,9},{5... | collective-permute-start | bytes 786440 | tf_op jit(solution)/shard_map/ppermute | solution.py:331
  29.9 4.3 %collective-permute-start.5 = (f32[1024,256]{1,0:T(8,128)S(1)}, f32[1024,256]{1,0:T(8,128)S(1)}, u32[]{:S(2)}, u32[]{:S(2)}) collective-permute-start(f32[1024,256]{1,0:T(8,128)S(1)} %cross.4), channel_id=1, source_target_pairs={{0,4},{4,0},{8,12},{12,8},{16,20},{20,16},{24,28},{28,24},{1,5},{5... | collective-permute-start | bytes 3145736 | tf_op jit(solution)/shard_map/ppermute | solution.py:326
  32.6 9.2 %collective-permute-start.4 = (f32[256,256]{1,0:T(8,128)S(1)}, f32[256,256]{1,0:T(8,128)S(1)}, u32[]{:S(2)}, u32[]{:S(2)}) collective-permute-start(f32[256,256]{1,0:T(8,128)S(1)} %add.53), channel_id=1, source_target_pairs={{0,16},{4,12},{8,24},{12,4},{16,0},{20,28},{24,8},{28,20},{1,17},{... | collective-permute-start | bytes 786440 | tf_op jit(solution)/shard_map/ppermute | solution.py:331
  34.2 14.1 %collective-permute-start.8 = (f32[512,256]{1,0:T(8,128)S(1)}, f32[512,256]{1,0:T(8,128)S(1)}, u32[]{:S(2)}, u32[]{:S(2)}) collective-permute-start(f32[512,256]{1,0:T(8,128)S(1)} %slice_add_fusion.1), channel_id=1, source_target_pairs={{0,8},{4,20},{8,0},{12,28},{16,24},{20,4},{24,16},{28,12},{1,9},{5... | collective-permute-start | bytes 1572872 | tf_op jit(solution)/shard_map/ppermute | solution.py:331
  38.0 3.9 %collective-permute-start.7 = (f32[1024,256]{1,0:T(8,128)S(1)}, f32[1024,256]{1,0:T(8,128)S(1)}, u32[]{:S(2)}, u32[]{:S(2)}) collective-permute-start(f32[1024,256]{1,0:T(8,128)S(1)} %cross.6), channel_id=1, source_target_pairs={{0,4},{4,0},{8,12},{12,8},{16,20},{20,16},{24,28},{28,24},{1,5},{5... | collective-permute-start | bytes 3145736 | tf_op jit(solution)/shard_map/ppermute | solution.py:326
  41.9 9.2 %collective-permute-start.9 = (f32[512,256]{1,0:T(8,128)S(1)}, f32[512,256]{1,0:T(8,128)S(1)}, u32[]{:S(2)}, u32[]{:S(2)}) collective-permute-start(f32[512,256]{1,0:T(8,128)S(1)} %slice_add_fusion), channel_id=1, source_target_pairs={{0,8},{4,20},{8,0},{12,28},{16,24},{20,4},{24,16},{28,12},{1,9},{5... | collective-permute-start | bytes 1572872 | tf_op jit(solution)/shard_map/ppermute | solution.py:331
  42.9 1.5 %collective-permute-start.6 = (f32[256,256]{1,0:T(8,128)S(1)}, f32[256,256]{1,0:T(8,128)S(1)}, u32[]{:S(2)}, u32[]{:S(2)}) collective-permute-start(f32[256,256]{1,0:T(8,128)S(1)} %add.55), channel_id=1, source_target_pairs={{0,4},{4,0},{8,12},{12,8},{16,20},{20,16},{24,28},{28,24},{1,5},{5... | collective-permute-start | bytes 786440 | tf_op jit(solution)/shard_map/ppermute | solution.py:326
  48.4 8.3 %collective-permute-start.10 = (f32[256,256]{1,0:T(8,128)S(1)}, f32[256,256]{1,0:T(8,128)S(1)}, u32[]{:S(2)}, u32[]{:S(2)}) collective-permute-start(f32[256,256]{1,0:T(8,128)S(1)} %slice_add_fusion.8), channel_id=1, source_target_pairs={{0,16},{4,12},{8,24},{12,4},{16,0},{20,28},{24,8},{28,20},{1,17},{... | collective-permute-start | bytes 786440 | tf_op jit(solution)/shard_map/ppermute | solution.py:331
  51.2 6.4 %collective-permute-start.11 = (f32[256,256]{1,0:T(8,128)S(1)}, f32[256,256]{1,0:T(8,128)S(1)}, u32[]{:S(2)}, u32[]{:S(2)}) collective-permute-start(f32[256,256]{1,0:T(8,128)S(1)} %slice_add_fusion.6), channel_id=1, source_target_pairs={{0,16},{4,12},{8,24},{12,4},{16,0},{20,28},{24,8},{28,20},{1,17},{... | collective-permute-start | bytes 786440 | tf_op jit(solution)/shard_map/ppermute | solution.py:331
  56.8 7.1 %collective-permute-start.13 = (f32[256,256]{1,0:T(8,128)S(1)}, f32[256,256]{1,0:T(8,128)S(1)}, u32[]{:S(2)}, u32[]{:S(2)}) collective-permute-start(f32[256,256]{1,0:T(8,128)S(1)} %fusion.3), channel_id=1, source_target_pairs={{0,16},{4,12},{8,24},{12,4},{16,0},{20,28},{24,8},{28,20},{1,17},{... | collective-permute-start | bytes 786440 | tf_op jit(solution)/shard_map/ppermute | solution.py:331
  57.8 8.3 %collective-permute-start.12 = (f32[256,256]{1,0:T(8,128)S(1)}, f32[256,256]{1,0:T(8,128)S(1)}, u32[]{:S(2)}, u32[]{:S(2)}) collective-permute-start(f32[256,256]{1,0:T(8,128)S(1)} %fusion.2), channel_id=1, source_target_pairs={{0,16},{4,12},{8,24},{12,4},{16,0},{20,28},{24,8},{28,20},{1,17},{... | collective-permute-start | bytes 786440 | tf_op jit(solution)/shard_map/ppermute | solution.py:331
  63.9 3.2 %collective-permute-start.17 = (f32[512,256]{1,0:T(8,128)S(1)}, f32[512,256]{1,0:T(8,128)S(1)}, u32[]{:S(2)}, u32[]{:S(2)}) collective-permute-start(f32[512,256]{1,0:T(8,128)S(1)} %pad_maximum_fusion.3.refs_0_), channel_id=1, source_target_pairs={{0,4},{4,0},{8,12},{12,8},{16,20},{20,16},{24,28},{28,24},{1,5},{5... | collective-permute-start | bytes 1572872 | tf_op jit(solution)/shard_map/ppermute | solution.py:326
  64.0 9.2 %collective-permute-start.16 = (f32[512,256]{1,0:T(8,128)S(1)}, f32[512,256]{1,0:T(8,128)S(1)}, u32[]{:S(2)}, u32[]{:S(2)}) collective-permute-start(f32[512,256]{1,0:T(8,128)S(1)} %pad_maximum_fusion.3.refs_0_), channel_id=1, source_target_pairs={{0,8},{4,20},{8,0},{12,28},{16,24},{20,4},{24,16},{28,12},{1,9},{5... | collective-permute-start | bytes 1572872 | tf_op jit(solution)/shard_map/ppermute | solution.py:331
  66.1 7.1 %collective-permute-start.15 = (f32[512,256]{1,0:T(8,128)S(1)}, f32[512,256]{1,0:T(8,128)S(1)}, u32[]{:S(2)}, u32[]{:S(2)}) collective-permute-start(f32[512,256]{1,0:T(8,128)S(1)} %pad_maximum_fusion.1.refs_2_), channel_id=1, source_target_pairs={{0,4},{4,0},{8,12},{12,8},{16,20},{20,16},{24,28},{28,24},{1,5},{5... | collective-permute-start | bytes 1572872 | tf_op jit(solution)/shard_map/ppermute | solution.py:326
  66.2 12.7 %collective-permute-start.14 = (f32[512,256]{1,0:T(8,128)S(1)}, f32[512,256]{1,0:T(8,128)S(1)}, u32[]{:S(2)}, u32[]{:S(2)}) collective-permute-start(f32[512,256]{1,0:T(8,128)S(1)} %pad_maximum_fusion.1.refs_2_), channel_id=1, source_target_pairs={{0,8},{4,20},{8,0},{12,28},{16,24},{20,4},{24,16},{28,12},{1,9},{5... | collective-permute-start | bytes 1572872 | tf_op jit(solution)/shard_map/ppermute | solution.py:331
  73.2 7.0 %collective-permute-start.18 = (f32[512,256]{1,0:T(8,128)S(1)}, f32[512,256]{1,0:T(8,128)S(1)}, u32[]{:S(2)}, u32[]{:S(2)}) collective-permute-start(f32[512,256]{1,0:T(8,128)S(1)} %collective-permute-done.16.refs_1_), channel_id=1, source_target_pairs={{0,4},{4,0},{8,12},{12,8},{16,20},{20,16},{24,28},{28,24},{1,5},{5... | collective-permute-start | bytes 1572872 | tf_op jit(solution)/shard_map/ppermute | solution.py:326
  78.8 1.9 %collective-permute-start.19 = (f32[512,256]{1,0:T(8,128)S(1)}, f32[512,256]{1,0:T(8,128)S(1)}, u32[]{:S(2)}, u32[]{:S(2)}) collective-permute-start(f32[512,256]{1,0:T(8,128)S(1)} %collective-permute-done.14.refs_1_), channel_id=1, source_target_pairs={{0,4},{4,0},{8,12},{12,8},{16,20},{20,16},{24,28},{28,24},{1,5},{5... | collective-permute-start | bytes 1572872 | tf_op jit(solution)/shard_map/ppermute | solution.py:326
where the time goes:
time: 86.2 us; the launch traced here: 85.6 us
  Pallas kernels  44.6 us (52%)
  starting transfers between devices  22.3 us (26%)
  waiting for transfers between devices  15 us (17%)
  matrix products  1.41 us (2%)
  other arithmetic  1.3 us (2%)
  between operations  1.04 us (1%)
    pallas_call x3, Pallas kernels, residual_call(): pl.pallas_call(functools.partial(residual_kernel, firsts, each), in_specs...  13.2 us
    ppermute x10, starting transfers between devices, exchange(): lax.ppermute(value, 'row', [(i, i ^ (bits[-1 - step] if i & 1 else bits[s...  12.7 us
    pallas_call x3, Pallas kernels, factor_call(): pl.pallas_call(body, out_shape=shapes, in_specs=in_specs, out_specs=[pl.B...  12.3 us
    pallas_call x4, Pallas kernels, cross_call(): pl.pallas_call(functools.partial(cross_kernel, first, each), in_specs=[pl...  10.4 us
    pallas_call x1, Pallas kernels, hold_call(): pl.pallas_call(hold_kernel, in_specs=[scalars, scalars, pl.BlockSpec(memo...  7.45 us
    ppermute x10, waiting for transfers between devices, exchange(): lax.ppermute(value, 'row', [(i, i ^ (bits[-1 - step] if i & 1 else bits[s...  6.62 us
    ppermute x1, waiting for transfers between devices, gather_panel(): above = [lax.ppermute(shard, 'col', up)]  6.07 us
    ppermute x1, starting transfers between devices, gather_panel(): above = [lax.ppermute(shard, 'col', up)]  5.1 us
  transfers between devices with their start and end apart: 20, of which 10 were waited for; matrix products, arithmetic and copies ran while one was open for 3% of the time, Pallas kernels for 45%

commit v1 on v0

--- a/solution.py
+++ b/solution.py
@@ -153,18 +153,19 @@
             sent.at[place, :, here], out_ref.at[rows, here], departures.at[place, part]
         )
 
-    for part, (first, total) in enumerate(zip(firsts, totals)):
-        high, low = split(total[...])
-        terms = jnp.concatenate([high, high, low], 1)
-        rows = [pl.ds(pl.multiple_of(table_ref[first + at], tile), tile) for at in range(each)]
-        for start in range(0, columns, chunk):
-            here = slice(start, start + chunk)
-            product = dot(terms, weight_ref[:, here], ((1,), (0,)))
-            for at in range(each):
-                window = window_high[rows[at], here].astype(f32)
-                window = window + window_low[rows[at], here].astype(f32)
-                sent[part * each + at, :, here] = window - product[at * tile : (at + 1) * tile]
-                leaving(part * each + at, first + at, start // chunk).start()
+    pairs = [split(total[...]) for total in totals]
+    high, low = [jnp.concatenate(term, 0) for term in zip(*pairs)]
+    terms = jnp.concatenate([high, high, low], 1)
+    entries = [first + at for first in firsts for at in range(each)]
+    rows = [pl.ds(pl.multiple_of(table_ref[at], tile), tile) for at in entries]
+    for start in range(0, columns, chunk):
+        here = slice(start, start + chunk)
+        product = dot(terms, weight_ref[:, here], ((1,), (0,)))
+        for place, entry in enumerate(entries):
+            window = window_high[rows[place], here].astype(f32)
+            window = window + window_low[rows[place], here].astype(f32)
+            sent[place, :, here] = window - product[place * tile : (place + 1) * tile]
+            leaving(place, entry, start // chunk).start()
 
     for part, first in enumerate(firsts):
         for at in range(each):
@@ -212,29 +213,28 @@
     ]
     inverse = [jnp.where(row_at[t] == lane_at, 1.0, 0.0) for t in range(tiles)]
     lower = [jnp.zeros((tile, lanes), f32) for _ in range(tiles)]
-    scale = [jnp.zeros((tile, lanes), f32) for _ in range(tiles)]
+    row_of = lambda parts, row: parts[row // tile][row % tile : row % tile + 1, :]
+    pivot = row_of(spread[0], 0)
     for j in range(size):
-        own, at = j // tile, j % tile
-        pivot = spread[j][own][at : at + 1, :]
-        reciprocal = 1.0 / pivot
+        own = j // tile
         root = lax.rsqrt(pivot)
-        inverse_row = inverse[own][at : at + 1, :]
-        factor = {}
+        if j + 1 < size:
+            entry = row_of(spread[j], j + 1) * root
+            pivot = row_of(spread[j + 1], j + 1) - entry * entry
+        inverse_row = row_of(inverse, j) * root
+        column = {t: spread[j][t] * root for t in range(own, tiles)}
+        below = dict(column)
+        below[own] = jnp.where(row_at[own] > j, column[own], 0.0)
+        lower[own] = jnp.where((lane_at == j) & (row_at[own] >= j), column[own], lower[own])
+        for t in range(own + 1, tiles):
+            lower[t] = jnp.where(lane_at == j, column[t], lower[t])
         for t in range(own, tiles):
-            column = spread[j][t]
-            factor[t] = column * reciprocal
-            if t == own:
-                factor[t] = jnp.where(row_at[t] > j, factor[t], 0.0)
-                scale[t] = jnp.where(row_at[t] == j, root, scale[t])
-                lower[t] = jnp.where((lane_at == j) & (row_at[t] >= j), column * root, lower[t])
-            else:
-                lower[t] = jnp.where(lane_at == j, column * root, lower[t])
-            inverse[t] = inverse[t] - factor[t] * inverse_row
+            inverse[t] = inverse[t] - below[t] * inverse_row
+        inverse[own] = jnp.where(row_at[own] == j, inverse_row, inverse[own])
         for k in range(j + 1, size):
-            entry = spread[j][k // tile][k % tile : k % tile + 1, :]
+            entry = row_of(column, k)
             for t in range(k // tile, tiles):
-                spread[k][t] = spread[k][t] - factor[t] * entry
-    inverse = [inverse[t] * scale[t] for t in range(tiles)]
+                spread[k][t] = spread[k][t] - below[t] * entry
     return jnp.concatenate(lower, 0), jnp.concatenate(inverse, 0)
 
 

time: 86.2 us -> 85.8 us (level)
    pallas_call x3, Pallas kernels: 12.3 us -> 11 us  [factor_call(): pl.pallas_call(body, out_shape=shapes, in_specs=in_specs, out_specs=[pl.B...]
  transfers between devices with their start and end apart: 20 -> 20, of which waited for: 10 -> 10; matrix products, arithmetic and copies ran while one was open for 3% -> 3% of each run, Pallas kernels for 45% -> 44%
where the time goes in v1:
time: 85.8 us; the launch traced here: 85.2 us
  Pallas kernels  44.2 us (52%)
  starting transfers between devices  21.9 us (26%)
  waiting for transfers between devices  15.4 us (18%)
  matrix products  1.41 us (2%)
  other arithmetic  1.3 us (2%)
  between operations  1.05 us (1%)
    pallas_call x3, Pallas kernels, residual_call(): pl.pallas_call(functools.partial(residual_kernel, firsts, each), in_specs...  14 us
    ppermute x10, starting transfers between devices, exchange(): lax.ppermute(value, 'row', [(i, i ^ (bits[-1 - step] if i & 1 else bits[s...  12.3 us
    pallas_call x3, Pallas kernels, factor_call(): pl.pallas_call(body, out_shape=shapes, in_specs=in_specs, out_specs=[pl.B...  11 us
    pallas_call x4, Pallas kernels, cross_call(): pl.pallas_call(functools.partial(cross_kernel, first, each), in_specs=[pl...  10.4 us
    pallas_call x1, Pallas kernels, hold_call(): pl.pallas_call(hold_kernel, in_specs=[scalars, scalars, pl.BlockSpec(memo...  7.45 us
    ppermute x10, waiting for transfers between devices, exchange(): lax.ppermute(value, 'row', [(i, i ^ (bits[-1 - step] if i & 1 else bits[s...  6.98 us
    ppermute x1, waiting for transfers between devices, gather_panel(): above = [lax.ppermute(shard, 'col', up)]  6.07 us
    ppermute x1, starting transfers between devices, gather_panel(): above = [lax.ppermute(shard, 'col', up)]  5.1 us
  transfers between devices with their start and end apart: 20, of which 10 were waited for; matrix products, arithmetic and copies ran while one was open for 3% of the time, Pallas kernels for 44%

profile of v1, /device:TPU:0, one launch (start us, length us, event | category | flops | bytes accessed | tf_op | source)
XLA Modules:
  0.0 85.2 jit_solution(6375612830220454201)
XLA Ops:
  0.6 5.1 %collective-permute-start = (f32[64,1024]{1,0:T(8,128)}, f32[64,1024]{1,0:T(8,128)S(1)}, u32[]{:S(2)}, u32[]{:S(2)}) collective-permute-start(f32[64,1024]{1,0:T(8,128)} %refs_0_.1), channel_id=1, source_target_pairs={{0,3},{1,0},{2,1},{3,2},{4,7},{5,4},{6,5},{7,6},{8,11},{9,8},{10,9... | collective-permute-start | bytes 786440 | tf_op jit(solution)/shard_map/ppermute | solution.py:359
  5.7 6.1 %collective-permute-done.refs_1_ = f32[64,1024]{1,0:T(8,128)S(1)} collective-permute-done((f32[64,1024]{1,0:T(8,128)}, f32[64,1024]{1,0:T(8,128)S(1)}, u32[]{:S(2)}, u32[]{:S(2)}) %collective-permute-start) | collective-permute-done | bytes 262176 | tf_op jit(solution)/shard_map/ppermute | solution.py:359
  12.0 4.0 %collective-permute-start.1 = (f32[64,1024]{1,0:T(8,128)S(1)}, f32[64,1024]{1,0:T(8,128)S(1)}, u32[]{:S(2)}, u32[]{:S(2)}) collective-permute-start(f32[64,1024]{1,0:T(8,128)S(1)} %collective-permute-done.refs_1_), channel_id=1, source_target_pairs={{0,3},{1,0},{2,1},{3,2},{4,7},{5,4},{6,5},{7,6},{8,11},{9,8},{10,9... | collective-permute-start | bytes 786440 | tf_op jit(solution)/shard_map/ppermute | solution.py:364
  16.0 0.7 broadcast_add_fusion.1
  16.7 7.4 %hold.1 = (bf16[4096,1024]{1,0:T(8,128)(2,1)S(1)}, bf16[4096,1024]{1,0:T(8,128)(2,1)S(1)}) custom-call(s32[16]{0:T(128)S(1)} %pad_add_fusion.table_ref, s32[1]{0:T(128)} %bitcast.place_ref, f32[4096,1024]{1,0:T(8,128)} %window_ref.1), custom_call_target="tpu_custom_call" | custom-call | flops 1 | bytes 1 | tf_op jit(solution)/shard_map/hold/pallas_call | solution.py:96
  24.5 1.3 %gram.1 = (f32[256,1024]{1,0:T(8,128)S(1)}, bf16[256,1024]{1,0:T(8,128)(2,1)S(1)}, bf16[256,1024]{1,0:T(8,128)(2,1)S(1)}, f32[256,256]{1,0:T(8,128)S(1)}) custom-call(s32[1]{0:T(128)} %bitcast.place_ref, f32[64,1024]{1,0:T(8,128)S(1)} %copy-done, f32[64,1024]{1,0:T(8,128)S(1)} %collective-permute-done.refs_1_, ...), custom_call_target="tpu_custom_call" | custom-call | flops 99999997952 | bytes 1 | tf_op jit(solution)/shard_map/gram/pallas_call | solution.py:49
  25.7 1.6 %collective-permute-start.3 = (f32[256,256]{1,0:T(8,128)S(1)}, f32[256,256]{1,0:T(8,128)S(1)}, u32[]{:S(2)}, u32[]{:S(2)}) collective-permute-start(f32[256,256]{1,0:T(8,128)S(1)} %get-tuple-element.42), channel_id=1, source_target_pairs={{0,8},{4,20},{8,0},{12,28},{16,24},{20,4},{24,16},{28,12},{1,9},{5... | collective-permute-start | bytes 786440 | tf_op jit(solution)/shard_map/ppermute | solution.py:331
  27.3 2.6 %cross.4 = f32[1024,256]{1,0:T(8,128)S(1)} custom-call(s32[16]{0:T(128)S(1)} %pad_add_fusion.table_ref, bf16[4096,1024]{1,0:T(8,128)(2,1)S(1)} %get-tuple-element.39.window_high, bf16[4096,1024]{1,0:T(8,128)(2,1)S(1)} %get-tuple-element.44.window_low, bf16[256,1024]{1,0:T(8,128)(2,1)S(1)} %get-tuple-element.45.high_ref, ...), custom_call_target="tpu_custom_call" | custom-call | flops 1 | bytes 1 | tf_op jit(solution)/shard_map/cross/pallas_call | solution.py:133
  30.0 2.6 %cross.5 = f32[1024,256]{1,0:T(8,128)S(1)} custom-call(s32[16]{0:T(128)S(1)} %pad_add_fusion.table_ref, bf16[4096,1024]{1,0:T(8,128)(2,1)S(1)} %get-tuple-element.39.window_high, bf16[4096,1024]{1,0:T(8,128)(2,1)S(1)} %get-tuple-element.44.window_low, bf16[256,1024]{1,0:T(8,128)(2,1)S(1)} %get-tuple-element.45.high_ref, ...), custom_call_target="tpu_custom_call" | custom-call | flops 99999997952 | bytes 1 | tf_op jit(solution)/shard_map/cross/pallas_call | solution.py:133
  32.6 1.6 %collective-permute-start.4 = (f32[256,256]{1,0:T(8,128)S(1)}, f32[256,256]{1,0:T(8,128)S(1)}, u32[]{:S(2)}, u32[]{:S(2)}) collective-permute-start(f32[256,256]{1,0:T(8,128)S(1)} %add.53), channel_id=1, source_target_pairs={{0,16},{4,12},{8,24},{12,4},{16,0},{20,28},{24,8},{28,20},{1,17},{... | collective-permute-start | bytes 786440 | tf_op jit(solution)/shard_map/ppermute | solution.py:331
  34.2 1.2 %collective-permute-start.8 = (f32[512,256]{1,0:T(8,128)S(1)}, f32[512,256]{1,0:T(8,128)S(1)}, u32[]{:S(2)}, u32[]{:S(2)}) collective-permute-start(f32[512,256]{1,0:T(8,128)S(1)} %slice_add_fusion.1), channel_id=1, source_target_pairs={{0,8},{4,20},{8,0},{12,28},{16,24},{20,4},{24,16},{28,12},{1,9},{5... | collective-permute-start | bytes 1572872 | tf_op jit(solution)/shard_map/ppermute | solution.py:331
  35.4 2.6 %cross.6 = f32[1024,256]{1,0:T(8,128)S(1)} custom-call(s32[16]{0:T(128)S(1)} %pad_add_fusion.table_ref, bf16[4096,1024]{1,0:T(8,128)(2,1)S(1)} %get-tuple-element.39.window_high, bf16[4096,1024]{1,0:T(8,128)(2,1)S(1)} %get-tuple-element.44.window_low, bf16[256,1024]{1,0:T(8,128)(2,1)S(1)} %get-tuple-element.45.high_ref, ...), custom_call_target="tpu_custom_call" | custom-call | flops 1 | bytes 1 | tf_op jit(solution)/shard_map/cross/pallas_call | solution.py:133
  38.1 2.7 %cross.7 = f32[1024,256]{1,0:T(8,128)S(1)} custom-call(s32[16]{0:T(128)S(1)} %pad_add_fusion.table_ref, bf16[4096,1024]{1,0:T(8,128)(2,1)S(1)} %get-tuple-element.39.window_high, bf16[4096,1024]{1,0:T(8,128)(2,1)S(1)} %get-tuple-element.44.window_low, bf16[256,1024]{1,0:T(8,128)(2,1)S(1)} %get-tuple-element.45.high_ref, ...), custom_call_target="tpu_custom_call" | custom-call | flops 99999997952 | bytes 1 | tf_op jit(solution)/shard_map/cross/pallas_call | solution.py:133
  40.8 1.0 %collective-permute-done.4 = f32[256,256]{1,0:T(8,128)S(1)} collective-permute-done((f32[256,256]{1,0:T(8,128)S(1)}, f32[256,256]{1,0:T(8,128)S(1)}, u32[]{:S(2)}, u32[]{:S(2)}) %collective-permute-start.4) | collective-permute-done | bytes 262176 | tf_op jit(solution)/shard_map/ppermute | solution.py:331
  41.9 0.9 %collective-permute-start.9 = (f32[512,256]{1,0:T(8,128)S(1)}, f32[512,256]{1,0:T(8,128)S(1)}, u32[]{:S(2)}, u32[]{:S(2)}) collective-permute-start(f32[512,256]{1,0:T(8,128)S(1)} %slice_add_fusion), channel_id=1, source_target_pairs={{0,8},{4,20},{8,0},{12,28},{16,24},{20,4},{24,16},{28,12},{1,9},{5... | collective-permute-start | bytes 1572872 | tf_op jit(solution)/shard_map/ppermute | solution.py:331
  42.9 1.5 %collective-permute-done.6 = f32[256,256]{1,0:T(8,128)S(1)} collective-permute-done((f32[256,256]{1,0:T(8,128)S(1)}, f32[256,256]{1,0:T(8,128)S(1)}, u32[]{:S(2)}, u32[]{:S(2)}) %collective-permute-start.6) | collective-permute-done | bytes 262176 | tf_op jit(solution)/shard_map/ppermute | solution.py:326
  44.4 3.7 %factor.3 = (f32[256,256]{1,0:T(8,128)S(1)}, f32[256,128]{1,0:T(8,128)S(1)}) custom-call(f32[256,256]{1,0:T(8,128)S(1)} %add.56.refs_0_), custom_call_target="tpu_custom_call" | custom-call | flops 1 | bytes 1 | tf_op jit(solution)/shard_map/factor/pallas_call | solution.py:314
  48.2 1.6 %collective-permute-start.10 = (f32[256,256]{1,0:T(8,128)S(1)}, f32[256,256]{1,0:T(8,128)S(1)}, u32[]{:S(2)}, u32[]{:S(2)}) collective-permute-start(f32[256,256]{1,0:T(8,128)S(1)} %slice_add_fusion.8), channel_id=1, source_target_pairs={{0,16},{4,12},{8,24},{12,4},{16,0},{20,28},{24,8},{28,20},{1,17},{... | collective-permute-start | bytes 786440 | tf_op jit(solution)/shard_map/ppermute | solution.py:331
  49.8 1.5 %collective-permute-done.9 = f32[512,256]{1,0:T(8,128)S(1)} collective-permute-done((f32[512,256]{1,0:T(8,128)S(1)}, f32[512,256]{1,0:T(8,128)S(1)}, u32[]{:S(2)}, u32[]{:S(2)}) %collective-permute-start.9) | collective-permute-done | bytes 524320 | tf_op jit(solution)/shard_map/ppermute | solution.py:331
  51.3 1.6 %collective-permute-start.11 = (f32[256,256]{1,0:T(8,128)S(1)}, f32[256,256]{1,0:T(8,128)S(1)}, u32[]{:S(2)}, u32[]{:S(2)}) collective-permute-start(f32[256,256]{1,0:T(8,128)S(1)} %slice_add_fusion.6), channel_id=1, source_target_pairs={{0,16},{4,12},{8,24},{12,4},{16,0},{20,28},{24,8},{28,20},{1,17},{... | collective-permute-start | bytes 786440 | tf_op jit(solution)/shard_map/ppermute | solution.py:331
  52.9 3.7 %factor.4 = (f32[256,256]{1,0:T(8,128)S(1)}, f32[256,128]{1,0:T(8,128)S(1)}) custom-call(f32[256,256]{1,0:T(8,128)S(1)} %get-tuple-element.57.refs_0_, f32[256,128]{1,0:T(8,128)S(1)} %get-tuple-element.58.refs_1_), custom_call_target="tpu_custom_call" | custom-call | flops 1 | bytes 1 | tf_op jit(solution)/shard_map/factor/pallas_call | solution.py:314
  56.7 0.6 collective-permute-start.13
  57.8 1.6 %collective-permute-start.12 = (f32[256,256]{1,0:T(8,128)S(1)}, f32[256,256]{1,0:T(8,128)S(1)}, u32[]{:S(2)}, u32[]{:S(2)}) collective-permute-start(f32[256,256]{1,0:T(8,128)S(1)} %fusion.2), channel_id=1, source_target_pairs={{0,16},{4,12},{8,24},{12,4},{16,0},{20,28},{24,8},{28,20},{1,17},{... | collective-permute-start | bytes 786440 | tf_op jit(solution)/shard_map/ppermute | solution.py:331
  59.4 3.7 %factor.5 = (f32[256,256]{1,0:T(8,128)}, f32[256,128]{1,0:T(8,128)}, f32[256,256]{1,0:T(8,128)}, f32[256,256]{1,0:T(8,128)S(1)}, bf16[768,1024]{1,0:T(8,128)(2,1)S(1)}) custom-call(f32[256,256]{1,0:T(8,128)S(1)} %get-tuple-element.62.refs_0_, f32[256,128]{1,0:T(8,128)S(1)} %get-tuple-element.63.refs_1_, f32[256,1024]{1,0:T(8,128)S(1)} %get-tuple-element.64.refs_2_), custom_call_target="tpu_custom_call" | custom-call | flops 1 | bytes 1 | tf_op jit(solution)/shard_map/factor/pallas_call | solution.py:314
  63.3 0.9 %collective-permute-start.16 = (f32[512,256]{1,0:T(8,128)S(1)}, f32[512,256]{1,0:T(8,128)S(1)}, u32[]{:S(2)}, u32[]{:S(2)}) collective-permute-start(f32[512,256]{1,0:T(8,128)S(1)} %pad_maximum_fusion.3.refs_0_), channel_id=1, source_target_pairs={{0,8},{4,20},{8,0},{12,28},{16,24},{20,4},{24,16},{28,12},{1,9},{5... | collective-permute-start | bytes 1572872 | tf_op jit(solution)/shard_map/ppermute | solution.py:331
  64.2 1.8 %collective-permute-done.12 = f32[256,256]{1,0:T(8,128)S(1)} collective-permute-done((f32[256,256]{1,0:T(8,128)S(1)}, f32[256,256]{1,0:T(8,128)S(1)}, u32[]{:S(2)}, u32[]{:S(2)}) %collective-permute-start.12) | collective-permute-done | bytes 262176 | tf_op jit(solution)/shard_map/ppermute | solution.py:331
  66.1 0.8 collective-permute-start.14
  66.9 5.3 %residual.3.refs_2_ = f32[4096,1024]{1,0:T(8,128)} custom-call(s32[16]{0:T(128)S(1)} %pad_add_fusion.table_ref, bf16[4096,1024]{1,0:T(8,128)(2,1)S(1)} %get-tuple-element.39.window_high, bf16[4096,1024]{1,0:T(8,128)(2,1)S(1)} %get-tuple-element.44.window_low, bf16[768,1024]{1,0:T(8,128)(2,1)S(1)} %get-tuple-element.66.weight_ref, ...), custom_call_target="tpu_custom_call" | custom-call | flops 1 | bytes 1 | tf_op jit(solution)/shard_map/residual/pallas_call | solution.py:186
  72.5 3.7 %residual.4.refs_3_ = f32[4096,1024]{1,0:T(8,128)} custom-call(s32[16]{0:T(128)S(1)} %pad_add_fusion.table_ref, bf16[4096,1024]{1,0:T(8,128)(2,1)S(1)} %get-tuple-element.39.window_high, bf16[4096,1024]{1,0:T(8,128)(2,1)S(1)} %get-tuple-element.44.window_low, bf16[768,1024]{1,0:T(8,128)(2,1)S(1)} %get-tuple-element.66.weight_ref, ...), custom_call_target="tpu_custom_call", output_to_operand_aliasing={{}: (6, {})} | custom-call | flops 1 | bytes 1 | tf_op jit(solution)/shard_map/residual/pallas_call | solution.py:186
  76.2 1.9 %collective-permute-done.14.refs_1_ = f32[512,256]{1,0:T(8,128)S(1)} collective-permute-done((f32[512,256]{1,0:T(8,128)S(1)}, f32[512,256]{1,0:T(8,128)S(1)}, u32[]{:S(2)}, u32[]{:S(2)}) %collective-permute-start.14) | collective-permute-done | bytes 524320 | tf_op jit(solution)/shard_map/ppermute | solution.py:331
  78.1 1.4 %fusion = f32[512,256]{1,0:T(8,128)} fusion(f32[256,256]{1,0:T(8,128)S(1)} %get-tuple-element.73, f32[256,256]{1,0:T(8,128)S(1)} %fusion.2, f32[256,256]{1,0:T(8,128)S(1)} %fusion.3), kind=kOutput, calls=%fused_computation.2 | convolution fusion | flops 402784256 | bytes 1310720 | tf_op jit(solution)/shard_map/dot_general | solution.py:20
  80.0 5.0 %residual.5 = f32[4096,1024]{1,0:T(8,128)} custom-call(s32[16]{0:T(128)S(1)} %pad_add_fusion.table_ref, bf16[4096,1024]{1,0:T(8,128)(2,1)S(1)} %get-tuple-element.39.window_high, bf16[4096,1024]{1,0:T(8,128)(2,1)S(1)} %get-tuple-element.44.window_low, bf16[768,1024]{1,0:T(8,128)(2,1)S(1)} %get-tuple-element.66.weight_ref, ...), custom_call_target="tpu_custom_call", output_to_operand_aliasing={{}: (7, {})} | custom-call | flops 1 | bytes 1 | tf_op jit(solution)/shard_map/residual/pallas_call | solution.py:186
  (36 shorter events, 2.7 us)
Async XLA Ops:
  0.6 23.9 %copy-start = (f32[64,1024]{1,0:T(8,128)S(1)}, f32[64,1024]{1,0:T(8,128)}, u32[]{:S(2)}) copy-start(f32[64,1024]{1,0:T(8,128)} %refs_0_.1) | copy-start | bytes 786436
  0.6 11.2 %collective-permute-start = (f32[64,1024]{1,0:T(8,128)}, f32[64,1024]{1,0:T(8,128)S(1)}, u32[]{:S(2)}, u32[]{:S(2)}) collective-permute-start(f32[64,1024]{1,0:T(8,128)} %refs_0_.1), channel_id=1, source_target_pairs={{0,3},{1,0},{2,1},{3,2},{4,7},{5,4},{6,5},{7,6},{8,11},{9,8},{10,9... | collective-permute-start | bytes 786440 | tf_op jit(solution)/shard_map/ppermute | solution.py:359
  11.8 12.4 %collective-permute-start.2 = (f32[64,1024]{1,0:T(8,128)}, f32[64,1024]{1,0:T(8,128)S(1)}, u32[]{:S(2)}, u32[]{:S(2)}) collective-permute-start(f32[64,1024]{1,0:T(8,128)} %refs_0_.1), channel_id=1, source_target_pairs={{0,1},{1,2},{2,3},{3,0},{4,5},{5,6},{6,7},{7,4},{8,9},{9,10},{10,1... | collective-permute-start | bytes 786440 | tf_op jit(solution)/shard_map/ppermute | solution.py:366
  12.0 12.5 %collective-permute-start.1 = (f32[64,1024]{1,0:T(8,128)S(1)}, f32[64,1024]{1,0:T(8,128)S(1)}, u32[]{:S(2)}, u32[]{:S(2)}) collective-permute-start(f32[64,1024]{1,0:T(8,128)S(1)} %collective-permute-done.refs_1_), channel_id=1, source_target_pairs={{0,3},{1,0},{2,1},{3,2},{4,7},{5,4},{6,5},{7,6},{8,11},{9,8},{10,9... | collective-permute-start | bytes 786440 | tf_op jit(solution)/shard_map/ppermute | solution.py:364
  25.7 6.8 %collective-permute-start.3 = (f32[256,256]{1,0:T(8,128)S(1)}, f32[256,256]{1,0:T(8,128)S(1)}, u32[]{:S(2)}, u32[]{:S(2)}) collective-permute-start(f32[256,256]{1,0:T(8,128)S(1)} %get-tuple-element.42), channel_id=1, source_target_pairs={{0,8},{4,20},{8,0},{12,28},{16,24},{20,4},{24,16},{28,12},{1,9},{5... | collective-permute-start | bytes 786440 | tf_op jit(solution)/shard_map/ppermute | solution.py:331
  29.9 4.3 %collective-permute-start.5 = (f32[1024,256]{1,0:T(8,128)S(1)}, f32[1024,256]{1,0:T(8,128)S(1)}, u32[]{:S(2)}, u32[]{:S(2)}) collective-permute-start(f32[1024,256]{1,0:T(8,128)S(1)} %cross.4), channel_id=1, source_target_pairs={{0,4},{4,0},{8,12},{12,8},{16,20},{20,16},{24,28},{28,24},{1,5},{5... | collective-permute-start | bytes 3145736 | tf_op jit(solution)/shard_map/ppermute | solution.py:326
  32.6 9.2 %collective-permute-start.4 = (f32[256,256]{1,0:T(8,128)S(1)}, f32[256,256]{1,0:T(8,128)S(1)}, u32[]{:S(2)}, u32[]{:S(2)}) collective-permute-start(f32[256,256]{1,0:T(8,128)S(1)} %add.53), channel_id=1, source_target_pairs={{0,16},{4,12},{8,24},{12,4},{16,0},{20,28},{24,8},{28,20},{1,17},{... | collective-permute-start | bytes 786440 | tf_op jit(solution)/shard_map/ppermute | solution.py:331
  34.2 13.9 %collective-permute-start.8 = (f32[512,256]{1,0:T(8,128)S(1)}, f32[512,256]{1,0:T(8,128)S(1)}, u32[]{:S(2)}, u32[]{:S(2)}) collective-permute-start(f32[512,256]{1,0:T(8,128)S(1)} %slice_add_fusion.1), channel_id=1, source_target_pairs={{0,8},{4,20},{8,0},{12,28},{16,24},{20,4},{24,16},{28,12},{1,9},{5... | collective-permute-start | bytes 1572872 | tf_op jit(solution)/shard_map/ppermute | solution.py:331
  38.0 3.9 %collective-permute-start.7 = (f32[1024,256]{1,0:T(8,128)S(1)}, f32[1024,256]{1,0:T(8,128)S(1)}, u32[]{:S(2)}, u32[]{:S(2)}) collective-permute-start(f32[1024,256]{1,0:T(8,128)S(1)} %cross.6), channel_id=1, source_target_pairs={{0,4},{4,0},{8,12},{12,8},{16,20},{20,16},{24,28},{28,24},{1,5},{5... | collective-permute-start | bytes 3145736 | tf_op jit(solution)/shard_map/ppermute | solution.py:326
  41.9 9.3 %collective-permute-start.9 = (f32[512,256]{1,0:T(8,128)S(1)}, f32[512,256]{1,0:T(8,128)S(1)}, u32[]{:S(2)}, u32[]{:S(2)}) collective-permute-start(f32[512,256]{1,0:T(8,128)S(1)} %slice_add_fusion), channel_id=1, source_target_pairs={{0,8},{4,20},{8,0},{12,28},{16,24},{20,4},{24,16},{28,12},{1,9},{5... | collective-permute-start | bytes 1572872 | tf_op jit(solution)/shard_map/ppermute | solution.py:331
  42.9 1.5 %collective-permute-start.6 = (f32[256,256]{1,0:T(8,128)S(1)}, f32[256,256]{1,0:T(8,128)S(1)}, u32[]{:S(2)}, u32[]{:S(2)}) collective-permute-start(f32[256,256]{1,0:T(8,128)S(1)} %add.55), channel_id=1, source_target_pairs={{0,4},{4,0},{8,12},{12,8},{16,20},{20,16},{24,28},{28,24},{1,5},{5... | collective-permute-start | bytes 786440 | tf_op jit(solution)/shard_map/ppermute | solution.py:326
  48.2 8.4 %collective-permute-start.10 = (f32[256,256]{1,0:T(8,128)S(1)}, f32[256,256]{1,0:T(8,128)S(1)}, u32[]{:S(2)}, u32[]{:S(2)}) collective-permute-start(f32[256,256]{1,0:T(8,128)S(1)} %slice_add_fusion.8), channel_id=1, source_target_pairs={{0,16},{4,12},{8,24},{12,4},{16,0},{20,28},{24,8},{28,20},{1,17},{... | collective-permute-start | bytes 786440 | tf_op jit(solution)/shard_map/ppermute | solution.py:331
  51.3 6.4 %collective-permute-start.11 = (f32[256,256]{1,0:T(8,128)S(1)}, f32[256,256]{1,0:T(8,128)S(1)}, u32[]{:S(2)}, u32[]{:S(2)}) collective-permute-start(f32[256,256]{1,0:T(8,128)S(1)} %slice_add_fusion.6), channel_id=1, source_target_pairs={{0,16},{4,12},{8,24},{12,4},{16,0},{20,28},{24,8},{28,20},{1,17},{... | collective-permute-start | bytes 786440 | tf_op jit(solution)/shard_map/ppermute | solution.py:331
  56.7 6.4 %collective-permute-start.13 = (f32[256,256]{1,0:T(8,128)S(1)}, f32[256,256]{1,0:T(8,128)S(1)}, u32[]{:S(2)}, u32[]{:S(2)}) collective-permute-start(f32[256,256]{1,0:T(8,128)S(1)} %fusion.3), channel_id=1, source_target_pairs={{0,16},{4,12},{8,24},{12,4},{16,0},{20,28},{24,8},{28,20},{1,17},{... | collective-permute-start | bytes 786440 | tf_op jit(solution)/shard_map/ppermute | solution.py:331
  57.8 8.1 %collective-permute-start.12 = (f32[256,256]{1,0:T(8,128)S(1)}, f32[256,256]{1,0:T(8,128)S(1)}, u32[]{:S(2)}, u32[]{:S(2)}) collective-permute-start(f32[256,256]{1,0:T(8,128)S(1)} %fusion.2), channel_id=1, source_target_pairs={{0,16},{4,12},{8,24},{12,4},{16,0},{20,28},{24,8},{28,20},{1,17},{... | collective-permute-start | bytes 786440 | tf_op jit(solution)/shard_map/ppermute | solution.py:331
  63.2 3.7 %collective-permute-start.17 = (f32[512,256]{1,0:T(8,128)S(1)}, f32[512,256]{1,0:T(8,128)S(1)}, u32[]{:S(2)}, u32[]{:S(2)}) collective-permute-start(f32[512,256]{1,0:T(8,128)S(1)} %pad_maximum_fusion.3.refs_0_), channel_id=1, source_target_pairs={{0,4},{4,0},{8,12},{12,8},{16,20},{20,16},{24,28},{28,24},{1,5},{5... | collective-permute-start | bytes 1572872 | tf_op jit(solution)/shard_map/ppermute | solution.py:326
  63.3 9.2 %collective-permute-start.16 = (f32[512,256]{1,0:T(8,128)S(1)}, f32[512,256]{1,0:T(8,128)S(1)}, u32[]{:S(2)}, u32[]{:S(2)}) collective-permute-start(f32[512,256]{1,0:T(8,128)S(1)} %pad_maximum_fusion.3.refs_0_), channel_id=1, source_target_pairs={{0,8},{4,20},{8,0},{12,28},{16,24},{20,4},{24,16},{28,12},{1,9},{5... | collective-permute-start | bytes 1572872 | tf_op jit(solution)/shard_map/ppermute | solution.py:331
  66.0 6.5 %collective-permute-start.15 = (f32[512,256]{1,0:T(8,128)S(1)}, f32[512,256]{1,0:T(8,128)S(1)}, u32[]{:S(2)}, u32[]{:S(2)}) collective-permute-start(f32[512,256]{1,0:T(8,128)S(1)} %pad_maximum_fusion.1.refs_2_), channel_id=1, source_target_pairs={{0,4},{4,0},{8,12},{12,8},{16,20},{20,16},{24,28},{28,24},{1,5},{5... | collective-permute-start | bytes 1572872 | tf_op jit(solution)/shard_map/ppermute | solution.py:326
  66.1 12.1 %collective-permute-start.14 = (f32[512,256]{1,0:T(8,128)S(1)}, f32[512,256]{1,0:T(8,128)S(1)}, u32[]{:S(2)}, u32[]{:S(2)}) collective-permute-start(f32[512,256]{1,0:T(8,128)S(1)} %pad_maximum_fusion.1.refs_2_), channel_id=1, source_target_pairs={{0,8},{4,20},{8,0},{12,28},{16,24},{20,4},{24,16},{28,12},{1,9},{5... | collective-permute-start | bytes 1572872 | tf_op jit(solution)/shard_map/ppermute | solution.py:331
  72.5 7.0 %collective-permute-start.18 = (f32[512,256]{1,0:T(8,128)S(1)}, f32[512,256]{1,0:T(8,128)S(1)}, u32[]{:S(2)}, u32[]{:S(2)}) collective-permute-start(f32[512,256]{1,0:T(8,128)S(1)} %collective-permute-done.16.refs_1_), channel_id=1, source_target_pairs={{0,4},{4,0},{8,12},{12,8},{16,20},{20,16},{24,28},{28,24},{1,5},{5... | collective-permute-start | bytes 1572872 | tf_op jit(solution)/shard_map/ppermute | solution.py:326
  78.1 1.9 %collective-permute-start.19 = (f32[512,256]{1,0:T(8,128)S(1)}, f32[512,256]{1,0:T(8,128)S(1)}, u32[]{:S(2)}, u32[]{:S(2)}) collective-permute-start(f32[512,256]{1,0:T(8,128)S(1)} %collective-permute-done.14.refs_1_), channel_id=1, source_target_pairs={{0,4},{4,0},{8,12},{12,8},{16,20},{20,16},{24,28},{28,24},{1,5},{5... | collective-permute-start | bytes 1572872 | tf_op jit(solution)/shard_map/ppermute | solution.py:326

commit v2 on v1

--- a/solution.py
+++ b/solution.py
@@ -39,7 +39,7 @@
         whole_ref[pl.ds(pl.multiple_of(owner * rows, rows), rows), :] = shard[...]
     whole = whole_ref[...]
     gram_ref[...] = dot(whole, whole, ((1,), (1,)), precise)
-    high_ref[...], low_ref[...] = split(whole)
+    high_ref[...], low_ref[...] = split(whole.T)
 
 
 def gram_call(place, shards):
@@ -52,8 +52,8 @@
         out_specs=[in_vmem] * 4,
         out_shape=[
             jax.ShapeDtypeStruct((panel, columns), f32),
-            jax.ShapeDtypeStruct((panel, columns), bf16),
-            jax.ShapeDtypeStruct((panel, columns), bf16),
+            jax.ShapeDtypeStruct((columns, panel), bf16),
+            jax.ShapeDtypeStruct((columns, panel), bf16),
             jax.ShapeDtypeStruct((panel, panel), f32),
         ],
         compiler_params=pltpu.CompilerParams(vmem_limit_bytes=24 * MIB),
@@ -110,7 +110,7 @@
 
 def cross_kernel(first, each, table_ref, window_high, window_low, high_ref, low_ref, *outs):
     tile = outs[0].shape[0] // each
-    dims = ((1,), (1,))
+    dims = ((1,), (0,))
     pair = 3 - len(outs) if each % 2 == 0 else 1
 
     @pl.loop(0, each // pair)
@@ -134,7 +134,7 @@
         functools.partial(cross_kernel, first, each),
         in_specs=[pl.BlockSpec(memory_space=pltpu.SMEM)] + [in_vmem] * 4,
         out_specs=[in_vmem] * parts,
-        out_shape=[jax.ShapeDtypeStruct((each * tile, panel[0].shape[0]), f32)] * parts,
+        out_shape=[jax.ShapeDtypeStruct((each * tile, panel[0].shape[1]), f32)] * parts,
         compiler_params=pltpu.CompilerParams(vmem_limit_bytes=ROOM),
         cost_estimate=cost,
         name="cross",
@@ -153,19 +153,18 @@
             sent.at[place, :, here], out_ref.at[rows, here], departures.at[place, part]
         )
 
-    pairs = [split(total[...]) for total in totals]
-    high, low = [jnp.concatenate(term, 0) for term in zip(*pairs)]
-    terms = jnp.concatenate([high, high, low], 1)
-    entries = [first + at for first in firsts for at in range(each)]
-    rows = [pl.ds(pl.multiple_of(table_ref[at], tile), tile) for at in entries]
-    for start in range(0, columns, chunk):
-        here = slice(start, start + chunk)
-        product = dot(terms, weight_ref[:, here], ((1,), (0,)))
-        for place, entry in enumerate(entries):
-            window = window_high[rows[place], here].astype(f32)
-            window = window + window_low[rows[place], here].astype(f32)
-            sent[place, :, here] = window - product[place * tile : (place + 1) * tile]
-            leaving(place, entry, start // chunk).start()
+    for part, (first, total) in enumerate(zip(firsts, totals)):
+        high, low = split(total[...])
+        terms = jnp.concatenate([high, high, low], 1)
+        rows = [pl.ds(pl.multiple_of(table_ref[first + at], tile), tile) for at in range(each)]
+        for start in range(0, columns, chunk):
+            here = slice(start, start + chunk)
+            product = dot(terms, weight_ref[:, here], ((1,), (0,)))
+            for at in range(each):
+                window = window_high[rows[at], here].astype(f32)
+                window = window + window_low[rows[at], here].astype(f32)
+                sent[part * each + at, :, here] = window - product[at * tile : (at + 1) * tile]
+                leaving(part * each + at, first + at, start // chunk).start()
 
     for part, first in enumerate(firsts):
         for at in range(each):

time: 85.8 us -> 85.2 us (level)
  Pallas kernels: 44.2 us -> 43 us
  starting transfers between devices: 21.9 us -> 22.9 us
    ppermute x10, starting transfers between devices: 12.3 us -> 13.4 us  [exchange(): lax.ppermute(value, 'row', [(i, i ^ (bits[-1 - step] if i & 1 else bits[s...]
    pallas_call x3, Pallas kernels: 14 us -> 13.1 us  [residual_call(): pl.pallas_call(functools.partial(residual_kernel, firsts, each), in_specs...]
where the time goes in v2:
time: 85.2 us; the launch traced here: 84.6 us
  Pallas kernels  43 us (50%)
  starting transfers between devices  22.9 us (27%)
  waiting for transfers between devices  14.9 us (17%)
  matrix products  1.41 us (2%)
  other arithmetic  1.31 us (2%)
  between operations  1.06 us (1%)
    ppermute x10, starting transfers between devices, exchange(): lax.ppermute(value, 'row', [(i, i ^ (bits[-1 - step] if i & 1 else bits[s...  13.4 us
    pallas_call x3, Pallas kernels, residual_call(): pl.pallas_call(functools.partial(residual_kernel, firsts, each), in_specs...  13.1 us
    pallas_call x3, Pallas kernels, factor_call(): pl.pallas_call(body, out_shape=shapes, in_specs=in_specs, out_specs=[pl.B...  11.1 us
    pallas_call x4, Pallas kernels, cross_call(): pl.pallas_call(functools.partial(cross_kernel, first, each), in_specs=[pl...  10.2 us
    pallas_call x1, Pallas kernels, hold_call(): pl.pallas_call(hold_kernel, in_specs=[scalars, scalars, pl.BlockSpec(memo...  7.45 us
    ppermute x10, waiting for transfers between devices, exchange(): lax.ppermute(value, 'row', [(i, i ^ (bits[-1 - step] if i & 1 else bits[s...  6.51 us
    ppermute x1, waiting for transfers between devices, gather_panel(): above = [lax.ppermute(shard, 'col', up)]  6.07 us
    ppermute x1, starting transfers between devices, gather_panel(): above = [lax.ppermute(shard, 'col', up)]  5.1 us
  transfers between devices with their start and end apart: 20, of which 10 were waited for; matrix products, arithmetic and copies ran while one was open for 3% of the time, Pallas kernels for 44%

profile of v2, /device:TPU:0, one launch (start us, length us, event | category | flops | bytes accessed | tf_op | source)
XLA Modules:
  0.0 84.6 jit_solution(10632322449796356878)
XLA Ops:
  0.6 5.1 %collective-permute-start = (f32[64,1024]{1,0:T(8,128)}, f32[64,1024]{1,0:T(8,128)S(1)}, u32[]{:S(2)}, u32[]{:S(2)}) collective-permute-start(f32[64,1024]{1,0:T(8,128)} %refs_0_.1), channel_id=1, source_target_pairs={{0,3},{1,0},{2,1},{3,2},{4,7},{5,4},{6,5},{7,6},{8,11},{9,8},{10,9... | collective-permute-start | bytes 786440 | tf_op jit(solution)/shard_map/ppermute | solution.py:358
  5.7 6.1 %collective-permute-done.refs_1_ = f32[64,1024]{1,0:T(8,128)S(1)} collective-permute-done((f32[64,1024]{1,0:T(8,128)}, f32[64,1024]{1,0:T(8,128)S(1)}, u32[]{:S(2)}, u32[]{:S(2)}) %collective-permute-start) | collective-permute-done | bytes 262176 | tf_op jit(solution)/shard_map/ppermute | solution.py:358
  12.0 4.0 %collective-permute-start.1 = (f32[64,1024]{1,0:T(8,128)S(1)}, f32[64,1024]{1,0:T(8,128)S(1)}, u32[]{:S(2)}, u32[]{:S(2)}) collective-permute-start(f32[64,1024]{1,0:T(8,128)S(1)} %collective-permute-done.refs_1_), channel_id=1, source_target_pairs={{0,3},{1,0},{2,1},{3,2},{4,7},{5,4},{6,5},{7,6},{8,11},{9,8},{10,9... | collective-permute-start | bytes 786440 | tf_op jit(solution)/shard_map/ppermute | solution.py:363
  16.0 0.7 broadcast_add_fusion.1
  16.7 7.4 %hold.1 = (bf16[4096,1024]{1,0:T(8,128)(2,1)S(1)}, bf16[4096,1024]{1,0:T(8,128)(2,1)S(1)}) custom-call(s32[16]{0:T(128)S(1)} %pad_add_fusion.table_ref, s32[1]{0:T(128)} %bitcast.place_ref, f32[4096,1024]{1,0:T(8,128)} %window_ref.1), custom_call_target="tpu_custom_call" | custom-call | flops 1 | bytes 1 | tf_op jit(solution)/shard_map/hold/pallas_call | solution.py:96
  24.5 1.2 %gram.1 = (f32[256,1024]{1,0:T(8,128)S(1)}, bf16[1024,256]{1,0:T(8,128)(2,1)S(1)}, bf16[1024,256]{1,0:T(8,128)(2,1)S(1)}, f32[256,256]{1,0:T(8,128)S(1)}) custom-call(s32[1]{0:T(128)} %bitcast.place_ref, f32[64,1024]{1,0:T(8,128)S(1)} %copy-done, f32[64,1024]{1,0:T(8,128)S(1)} %collective-permute-done.refs_1_, ...), custom_call_target="tpu_custom_call" | custom-call | flops 99999997952 | bytes 1 | tf_op jit(solution)/shard_map/gram/pallas_call | solution.py:49
  25.7 1.6 %collective-permute-start.3 = (f32[256,256]{1,0:T(8,128)S(1)}, f32[256,256]{1,0:T(8,128)S(1)}, u32[]{:S(2)}, u32[]{:S(2)}) collective-permute-start(f32[256,256]{1,0:T(8,128)S(1)} %get-tuple-element.42), channel_id=1, source_target_pairs={{0,8},{4,20},{8,0},{12,28},{16,24},{20,4},{24,16},{28,12},{1,9},{5... | collective-permute-start | bytes 786440 | tf_op jit(solution)/shard_map/ppermute | solution.py:330
  27.3 2.5 %cross.4 = f32[1024,256]{1,0:T(8,128)S(1)} custom-call(s32[16]{0:T(128)S(1)} %pad_add_fusion.table_ref, bf16[4096,1024]{1,0:T(8,128)(2,1)S(1)} %get-tuple-element.39.window_high, bf16[4096,1024]{1,0:T(8,128)(2,1)S(1)} %get-tuple-element.44.window_low, bf16[1024,256]{1,0:T(8,128)(2,1)S(1)} %get-tuple-element.45.high_ref, ...), custom_call_target="tpu_custom_call" | custom-call | flops 1 | bytes 1 | tf_op jit(solution)/shard_map/cross/pallas_call | solution.py:133
  29.8 2.5 %cross.5 = f32[1024,256]{1,0:T(8,128)S(1)} custom-call(s32[16]{0:T(128)S(1)} %pad_add_fusion.table_ref, bf16[4096,1024]{1,0:T(8,128)(2,1)S(1)} %get-tuple-element.39.window_high, bf16[4096,1024]{1,0:T(8,128)(2,1)S(1)} %get-tuple-element.44.window_low, bf16[1024,256]{1,0:T(8,128)(2,1)S(1)} %get-tuple-element.45.high_ref, ...), custom_call_target="tpu_custom_call" | custom-call | flops 99999997952 | bytes 1 | tf_op jit(solution)/shard_map/cross/pallas_call | solution.py:133
  32.4 1.6 %collective-permute-start.4 = (f32[256,256]{1,0:T(8,128)S(1)}, f32[256,256]{1,0:T(8,128)S(1)}, u32[]{:S(2)}, u32[]{:S(2)}) collective-permute-start(f32[256,256]{1,0:T(8,128)S(1)} %add.53), channel_id=1, source_target_pairs={{0,16},{4,12},{8,24},{12,4},{16,0},{20,28},{24,8},{28,20},{1,17},{... | collective-permute-start | bytes 786440 | tf_op jit(solution)/shard_map/ppermute | solution.py:330
  34.1 1.3 %collective-permute-start.8 = (f32[512,256]{1,0:T(8,128)S(1)}, f32[512,256]{1,0:T(8,128)S(1)}, u32[]{:S(2)}, u32[]{:S(2)}) collective-permute-start(f32[512,256]{1,0:T(8,128)S(1)} %slice_add_fusion.1), channel_id=1, source_target_pairs={{0,8},{4,20},{8,0},{12,28},{16,24},{20,4},{24,16},{28,12},{1,9},{5... | collective-permute-start | bytes 1572872 | tf_op jit(solution)/shard_map/ppermute | solution.py:330
  35.4 2.5 %cross.6 = f32[1024,256]{1,0:T(8,128)S(1)} custom-call(s32[16]{0:T(128)S(1)} %pad_add_fusion.table_ref, bf16[4096,1024]{1,0:T(8,128)(2,1)S(1)} %get-tuple-element.39.window_high, bf16[4096,1024]{1,0:T(8,128)(2,1)S(1)} %get-tuple-element.44.window_low, bf16[1024,256]{1,0:T(8,128)(2,1)S(1)} %get-tuple-element.45.high_ref, ...), custom_call_target="tpu_custom_call" | custom-call | flops 1 | bytes 1 | tf_op jit(solution)/shard_map/cross/pallas_call | solution.py:133
  38.0 2.7 %cross.7 = f32[1024,256]{1,0:T(8,128)S(1)} custom-call(s32[16]{0:T(128)S(1)} %pad_add_fusion.table_ref, bf16[4096,1024]{1,0:T(8,128)(2,1)S(1)} %get-tuple-element.39.window_high, bf16[4096,1024]{1,0:T(8,128)(2,1)S(1)} %get-tuple-element.44.window_low, bf16[1024,256]{1,0:T(8,128)(2,1)S(1)} %get-tuple-element.45.high_ref, ...), custom_call_target="tpu_custom_call" | custom-call | flops 99999997952 | bytes 1 | tf_op jit(solution)/shard_map/cross/pallas_call | solution.py:133
  40.7 1.0 %collective-permute-done.4 = f32[256,256]{1,0:T(8,128)S(1)} collective-permute-done((f32[256,256]{1,0:T(8,128)S(1)}, f32[256,256]{1,0:T(8,128)S(1)}, u32[]{:S(2)}, u32[]{:S(2)}) %collective-permute-start.4) | collective-permute-done | bytes 262176 | tf_op jit(solution)/shard_map/ppermute | solution.py:330
  41.8 1.2 %collective-permute-start.9 = (f32[512,256]{1,0:T(8,128)S(1)}, f32[512,256]{1,0:T(8,128)S(1)}, u32[]{:S(2)}, u32[]{:S(2)}) collective-permute-start(f32[512,256]{1,0:T(8,128)S(1)} %slice_add_fusion), channel_id=1, source_target_pairs={{0,8},{4,20},{8,0},{12,28},{16,24},{20,4},{24,16},{28,12},{1,9},{5... | collective-permute-start | bytes 1572872 | tf_op jit(solution)/shard_map/ppermute | solution.py:330
  43.0 1.5 %collective-permute-done.6 = f32[256,256]{1,0:T(8,128)S(1)} collective-permute-done((f32[256,256]{1,0:T(8,128)S(1)}, f32[256,256]{1,0:T(8,128)S(1)}, u32[]{:S(2)}, u32[]{:S(2)}) %collective-permute-start.6) | collective-permute-done | bytes 262176 | tf_op jit(solution)/shard_map/ppermute | solution.py:325
  44.5 3.7 %factor.3 = (f32[256,256]{1,0:T(8,128)S(1)}, f32[256,128]{1,0:T(8,128)S(1)}) custom-call(f32[256,256]{1,0:T(8,128)S(1)} %add.56.refs_0_), custom_call_target="tpu_custom_call" | custom-call | flops 1 | bytes 1 | tf_op jit(solution)/shard_map/factor/pallas_call | solution.py:313
  48.3 1.6 %collective-permute-start.10 = (f32[256,256]{1,0:T(8,128)S(1)}, f32[256,256]{1,0:T(8,128)S(1)}, u32[]{:S(2)}, u32[]{:S(2)}) collective-permute-start(f32[256,256]{1,0:T(8,128)S(1)} %slice_add_fusion.8), channel_id=1, source_target_pairs={{0,16},{4,12},{8,24},{12,4},{16,0},{20,28},{24,8},{28,20},{1,17},{... | collective-permute-start | bytes 786440 | tf_op jit(solution)/shard_map/ppermute | solution.py:330
  49.9 1.1 %collective-permute-done.9 = f32[512,256]{1,0:T(8,128)S(1)} collective-permute-done((f32[512,256]{1,0:T(8,128)S(1)}, f32[512,256]{1,0:T(8,128)S(1)}, u32[]{:S(2)}, u32[]{:S(2)}) %collective-permute-start.9) | collective-permute-done | bytes 524320 | tf_op jit(solution)/shard_map/ppermute | solution.py:330
  51.1 1.6 %collective-permute-start.11 = (f32[256,256]{1,0:T(8,128)S(1)}, f32[256,256]{1,0:T(8,128)S(1)}, u32[]{:S(2)}, u32[]{:S(2)}) collective-permute-start(f32[256,256]{1,0:T(8,128)S(1)} %slice_add_fusion.6), channel_id=1, source_target_pairs={{0,16},{4,12},{8,24},{12,4},{16,0},{20,28},{24,8},{28,20},{1,17},{... | collective-permute-start | bytes 786440 | tf_op jit(solution)/shard_map/ppermute | solution.py:330
  52.7 3.7 %factor.4 = (f32[256,256]{1,0:T(8,128)S(1)}, f32[256,128]{1,0:T(8,128)S(1)}) custom-call(f32[256,256]{1,0:T(8,128)S(1)} %get-tuple-element.57.refs_0_, f32[256,128]{1,0:T(8,128)S(1)} %get-tuple-element.58.refs_1_), custom_call_target="tpu_custom_call" | custom-call | flops 1 | bytes 1 | tf_op jit(solution)/shard_map/factor/pallas_call | solution.py:313
  56.4 0.6 collective-permute-start.13
  57.6 1.6 %collective-permute-start.12 = (f32[256,256]{1,0:T(8,128)S(1)}, f32[256,256]{1,0:T(8,128)S(1)}, u32[]{:S(2)}, u32[]{:S(2)}) collective-permute-start(f32[256,256]{1,0:T(8,128)S(1)} %fusion.2), channel_id=1, source_target_pairs={{0,16},{4,12},{8,24},{12,4},{16,0},{20,28},{24,8},{28,20},{1,17},{... | collective-permute-start | bytes 786440 | tf_op jit(solution)/shard_map/ppermute | solution.py:330
  59.2 3.7 %factor.5 = (f32[256,256]{1,0:T(8,128)}, f32[256,128]{1,0:T(8,128)}, f32[256,256]{1,0:T(8,128)}, f32[256,256]{1,0:T(8,128)S(1)}, bf16[768,1024]{1,0:T(8,128)(2,1)S(1)}) custom-call(f32[256,256]{1,0:T(8,128)S(1)} %get-tuple-element.62.refs_0_, f32[256,128]{1,0:T(8,128)S(1)} %get-tuple-element.63.refs_1_, f32[256,1024]{1,0:T(8,128)S(1)} %get-tuple-element.64.refs_2_), custom_call_target="tpu_custom_call" | custom-call | flops 1 | bytes 1 | tf_op jit(solution)/shard_map/factor/pallas_call | solution.py:313
  63.0 1.2 %collective-permute-start.16 = (f32[512,256]{1,0:T(8,128)S(1)}, f32[512,256]{1,0:T(8,128)S(1)}, u32[]{:S(2)}, u32[]{:S(2)}) collective-permute-start(f32[512,256]{1,0:T(8,128)S(1)} %pad_maximum_fusion.3.refs_0_), channel_id=1, source_target_pairs={{0,8},{4,20},{8,0},{12,28},{16,24},{20,4},{24,16},{28,12},{1,9},{5... | collective-permute-start | bytes 1572872 | tf_op jit(solution)/shard_map/ppermute | solution.py:330
  64.2 1.5 %collective-permute-done.12 = f32[256,256]{1,0:T(8,128)S(1)} collective-permute-done((f32[256,256]{1,0:T(8,128)S(1)}, f32[256,256]{1,0:T(8,128)S(1)}, u32[]{:S(2)}, u32[]{:S(2)}) %collective-permute-start.12) | collective-permute-done | bytes 262176 | tf_op jit(solution)/shard_map/ppermute | solution.py:330
  65.8 1.2 %collective-permute-start.14 = (f32[512,256]{1,0:T(8,128)S(1)}, f32[512,256]{1,0:T(8,128)S(1)}, u32[]{:S(2)}, u32[]{:S(2)}) collective-permute-start(f32[512,256]{1,0:T(8,128)S(1)} %pad_maximum_fusion.1.refs_2_), channel_id=1, source_target_pairs={{0,8},{4,20},{8,0},{12,28},{16,24},{20,4},{24,16},{28,12},{1,9},{5... | collective-permute-start | bytes 1572872 | tf_op jit(solution)/shard_map/ppermute | solution.py:330
  67.0 4.9 %residual.3.refs_2_ = f32[4096,1024]{1,0:T(8,128)} custom-call(s32[16]{0:T(128)S(1)} %pad_add_fusion.table_ref, bf16[4096,1024]{1,0:T(8,128)(2,1)S(1)} %get-tuple-element.39.window_high, bf16[4096,1024]{1,0:T(8,128)(2,1)S(1)} %get-tuple-element.44.window_low, bf16[768,1024]{1,0:T(8,128)(2,1)S(1)} %get-tuple-element.66.weight_ref, ...), custom_call_target="tpu_custom_call" | custom-call | flops 1 | bytes 1 | tf_op jit(solution)/shard_map/residual/pallas_call | solution.py:185
  72.3 3.6 %residual.4.refs_3_ = f32[4096,1024]{1,0:T(8,128)} custom-call(s32[16]{0:T(128)S(1)} %pad_add_fusion.table_ref, bf16[4096,1024]{1,0:T(8,128)(2,1)S(1)} %get-tuple-element.39.window_high, bf16[4096,1024]{1,0:T(8,128)(2,1)S(1)} %get-tuple-element.44.window_low, bf16[768,1024]{1,0:T(8,128)(2,1)S(1)} %get-tuple-element.66.weight_ref, ...), custom_call_target="tpu_custom_call", output_to_operand_aliasing={{}: (6, {})} | custom-call | flops 1 | bytes 1 | tf_op jit(solution)/shard_map/residual/pallas_call | solution.py:185
  75.9 2.0 %collective-permute-done.14.refs_1_ = f32[512,256]{1,0:T(8,128)S(1)} collective-permute-done((f32[512,256]{1,0:T(8,128)S(1)}, f32[512,256]{1,0:T(8,128)S(1)}, u32[]{:S(2)}, u32[]{:S(2)}) %collective-permute-start.14) | collective-permute-done | bytes 524320 | tf_op jit(solution)/shard_map/ppermute | solution.py:330
  77.9 1.4 %fusion = f32[512,256]{1,0:T(8,128)} fusion(f32[256,256]{1,0:T(8,128)S(1)} %get-tuple-element.73, f32[256,256]{1,0:T(8,128)S(1)} %fusion.2, f32[256,256]{1,0:T(8,128)S(1)} %fusion.3), kind=kOutput, calls=%fused_computation.2 | convolution fusion | flops 402784256 | bytes 1310720 | tf_op jit(solution)/shard_map/dot_general | solution.py:20
  79.8 4.7 %residual.5 = f32[4096,1024]{1,0:T(8,128)} custom-call(s32[16]{0:T(128)S(1)} %pad_add_fusion.table_ref, bf16[4096,1024]{1,0:T(8,128)(2,1)S(1)} %get-tuple-element.39.window_high, bf16[4096,1024]{1,0:T(8,128)(2,1)S(1)} %get-tuple-element.44.window_low, bf16[768,1024]{1,0:T(8,128)(2,1)S(1)} %get-tuple-element.66.weight_ref, ...), custom_call_target="tpu_custom_call", output_to_operand_aliasing={{}: (7, {})} | custom-call | flops 1 | bytes 1 | tf_op jit(solution)/shard_map/residual/pallas_call | solution.py:185
  (36 shorter events, 2.8 us)
Async XLA Ops:
  0.6 23.9 %copy-start = (f32[64,1024]{1,0:T(8,128)S(1)}, f32[64,1024]{1,0:T(8,128)}, u32[]{:S(2)}) copy-start(f32[64,1024]{1,0:T(8,128)} %refs_0_.1) | copy-start | bytes 786436
  0.6 11.2 %collective-permute-start = (f32[64,1024]{1,0:T(8,128)}, f32[64,1024]{1,0:T(8,128)S(1)}, u32[]{:S(2)}, u32[]{:S(2)}) collective-permute-start(f32[64,1024]{1,0:T(8,128)} %refs_0_.1), channel_id=1, source_target_pairs={{0,3},{1,0},{2,1},{3,2},{4,7},{5,4},{6,5},{7,6},{8,11},{9,8},{10,9... | collective-permute-start | bytes 786440 | tf_op jit(solution)/shard_map/ppermute | solution.py:358
  11.8 12.4 %collective-permute-start.2 = (f32[64,1024]{1,0:T(8,128)}, f32[64,1024]{1,0:T(8,128)S(1)}, u32[]{:S(2)}, u32[]{:S(2)}) collective-permute-start(f32[64,1024]{1,0:T(8,128)} %refs_0_.1), channel_id=1, source_target_pairs={{0,1},{1,2},{2,3},{3,0},{4,5},{5,6},{6,7},{7,4},{8,9},{9,10},{10,1... | collective-permute-start | bytes 786440 | tf_op jit(solution)/shard_map/ppermute | solution.py:365
  12.0 12.5 %collective-permute-start.1 = (f32[64,1024]{1,0:T(8,128)S(1)}, f32[64,1024]{1,0:T(8,128)S(1)}, u32[]{:S(2)}, u32[]{:S(2)}) collective-permute-start(f32[64,1024]{1,0:T(8,128)S(1)} %collective-permute-done.refs_1_), channel_id=1, source_target_pairs={{0,3},{1,0},{2,1},{3,2},{4,7},{5,4},{6,5},{7,6},{8,11},{9,8},{10,9... | collective-permute-start | bytes 786440 | tf_op jit(solution)/shard_map/ppermute | solution.py:363
  25.7 6.7 %collective-permute-start.3 = (f32[256,256]{1,0:T(8,128)S(1)}, f32[256,256]{1,0:T(8,128)S(1)}, u32[]{:S(2)}, u32[]{:S(2)}) collective-permute-start(f32[256,256]{1,0:T(8,128)S(1)} %get-tuple-element.42), channel_id=1, source_target_pairs={{0,8},{4,20},{8,0},{12,28},{16,24},{20,4},{24,16},{28,12},{1,9},{5... | collective-permute-start | bytes 786440 | tf_op jit(solution)/shard_map/ppermute | solution.py:330
  29.8 4.2 %collective-permute-start.5 = (f32[1024,256]{1,0:T(8,128)S(1)}, f32[1024,256]{1,0:T(8,128)S(1)}, u32[]{:S(2)}, u32[]{:S(2)}) collective-permute-start(f32[1024,256]{1,0:T(8,128)S(1)} %cross.4), channel_id=1, source_target_pairs={{0,4},{4,0},{8,12},{12,8},{16,20},{20,16},{24,28},{28,24},{1,5},{5... | collective-permute-start | bytes 3145736 | tf_op jit(solution)/shard_map/ppermute | solution.py:325
  32.4 9.2 %collective-permute-start.4 = (f32[256,256]{1,0:T(8,128)S(1)}, f32[256,256]{1,0:T(8,128)S(1)}, u32[]{:S(2)}, u32[]{:S(2)}) collective-permute-start(f32[256,256]{1,0:T(8,128)S(1)} %add.53), channel_id=1, source_target_pairs={{0,16},{4,12},{8,24},{12,4},{16,0},{20,28},{24,8},{28,20},{1,17},{... | collective-permute-start | bytes 786440 | tf_op jit(solution)/shard_map/ppermute | solution.py:330
  34.1 14.2 %collective-permute-start.8 = (f32[512,256]{1,0:T(8,128)S(1)}, f32[512,256]{1,0:T(8,128)S(1)}, u32[]{:S(2)}, u32[]{:S(2)}) collective-permute-start(f32[512,256]{1,0:T(8,128)S(1)} %slice_add_fusion.1), channel_id=1, source_target_pairs={{0,8},{4,20},{8,0},{12,28},{16,24},{20,4},{24,16},{28,12},{1,9},{5... | collective-permute-start | bytes 1572872 | tf_op jit(solution)/shard_map/ppermute | solution.py:330
  37.9 3.8 %collective-permute-start.7 = (f32[1024,256]{1,0:T(8,128)S(1)}, f32[1024,256]{1,0:T(8,128)S(1)}, u32[]{:S(2)}, u32[]{:S(2)}) collective-permute-start(f32[1024,256]{1,0:T(8,128)S(1)} %cross.6), channel_id=1, source_target_pairs={{0,4},{4,0},{8,12},{12,8},{16,20},{20,16},{24,28},{28,24},{1,5},{5... | collective-permute-start | bytes 3145736 | tf_op jit(solution)/shard_map/ppermute | solution.py:325
  41.8 9.2 %collective-permute-start.9 = (f32[512,256]{1,0:T(8,128)S(1)}, f32[512,256]{1,0:T(8,128)S(1)}, u32[]{:S(2)}, u32[]{:S(2)}) collective-permute-start(f32[512,256]{1,0:T(8,128)S(1)} %slice_add_fusion), channel_id=1, source_target_pairs={{0,8},{4,20},{8,0},{12,28},{16,24},{20,4},{24,16},{28,12},{1,9},{5... | collective-permute-start | bytes 1572872 | tf_op jit(solution)/shard_map/ppermute | solution.py:330
  42.9 1.5 %collective-permute-start.6 = (f32[256,256]{1,0:T(8,128)S(1)}, f32[256,256]{1,0:T(8,128)S(1)}, u32[]{:S(2)}, u32[]{:S(2)}) collective-permute-start(f32[256,256]{1,0:T(8,128)S(1)} %add.55), channel_id=1, source_target_pairs={{0,4},{4,0},{8,12},{12,8},{16,20},{20,16},{24,28},{28,24},{1,5},{5... | collective-permute-start | bytes 786440 | tf_op jit(solution)/shard_map/ppermute | solution.py:325
  48.3 8.0 %collective-permute-start.10 = (f32[256,256]{1,0:T(8,128)S(1)}, f32[256,256]{1,0:T(8,128)S(1)}, u32[]{:S(2)}, u32[]{:S(2)}) collective-permute-start(f32[256,256]{1,0:T(8,128)S(1)} %slice_add_fusion.8), channel_id=1, source_target_pairs={{0,16},{4,12},{8,24},{12,4},{16,0},{20,28},{24,8},{28,20},{1,17},{... | collective-permute-start | bytes 786440 | tf_op jit(solution)/shard_map/ppermute | solution.py:330
  51.1 6.5 %collective-permute-start.11 = (f32[256,256]{1,0:T(8,128)S(1)}, f32[256,256]{1,0:T(8,128)S(1)}, u32[]{:S(2)}, u32[]{:S(2)}) collective-permute-start(f32[256,256]{1,0:T(8,128)S(1)} %slice_add_fusion.6), channel_id=1, source_target_pairs={{0,16},{4,12},{8,24},{12,4},{16,0},{20,28},{24,8},{28,20},{1,17},{... | collective-permute-start | bytes 786440 | tf_op jit(solution)/shard_map/ppermute | solution.py:330
  56.4 6.5 %collective-permute-start.13 = (f32[256,256]{1,0:T(8,128)S(1)}, f32[256,256]{1,0:T(8,128)S(1)}, u32[]{:S(2)}, u32[]{:S(2)}) collective-permute-start(f32[256,256]{1,0:T(8,128)S(1)} %fusion.3), channel_id=1, source_target_pairs={{0,16},{4,12},{8,24},{12,4},{16,0},{20,28},{24,8},{28,20},{1,17},{... | collective-permute-start | bytes 786440 | tf_op jit(solution)/shard_map/ppermute | solution.py:330
  57.6 8.0 %collective-permute-start.12 = (f32[256,256]{1,0:T(8,128)S(1)}, f32[256,256]{1,0:T(8,128)S(1)}, u32[]{:S(2)}, u32[]{:S(2)}) collective-permute-start(f32[256,256]{1,0:T(8,128)S(1)} %fusion.2), channel_id=1, source_target_pairs={{0,16},{4,12},{8,24},{12,4},{16,0},{20,28},{24,8},{28,20},{1,17},{... | collective-permute-start | bytes 786440 | tf_op jit(solution)/shard_map/ppermute | solution.py:330
  62.9 4.1 %collective-permute-start.17 = (f32[512,256]{1,0:T(8,128)S(1)}, f32[512,256]{1,0:T(8,128)S(1)}, u32[]{:S(2)}, u32[]{:S(2)}) collective-permute-start(f32[512,256]{1,0:T(8,128)S(1)} %pad_maximum_fusion.3.refs_0_), channel_id=1, source_target_pairs={{0,4},{4,0},{8,12},{12,8},{16,20},{20,16},{24,28},{28,24},{1,5},{5... | collective-permute-start | bytes 1572872 | tf_op jit(solution)/shard_map/ppermute | solution.py:325
  63.0 9.2 %collective-permute-start.16 = (f32[512,256]{1,0:T(8,128)S(1)}, f32[512,256]{1,0:T(8,128)S(1)}, u32[]{:S(2)}, u32[]{:S(2)}) collective-permute-start(f32[512,256]{1,0:T(8,128)S(1)} %pad_maximum_fusion.3.refs_0_), channel_id=1, source_target_pairs={{0,8},{4,20},{8,0},{12,28},{16,24},{20,4},{24,16},{28,12},{1,9},{5... | collective-permute-start | bytes 1572872 | tf_op jit(solution)/shard_map/ppermute | solution.py:330
  65.7 6.6 %collective-permute-start.15 = (f32[512,256]{1,0:T(8,128)S(1)}, f32[512,256]{1,0:T(8,128)S(1)}, u32[]{:S(2)}, u32[]{:S(2)}) collective-permute-start(f32[512,256]{1,0:T(8,128)S(1)} %pad_maximum_fusion.1.refs_2_), channel_id=1, source_target_pairs={{0,4},{4,0},{8,12},{12,8},{16,20},{20,16},{24,28},{28,24},{1,5},{5... | collective-permute-start | bytes 1572872 | tf_op jit(solution)/shard_map/ppermute | solution.py:325
  65.8 12.1 %collective-permute-start.14 = (f32[512,256]{1,0:T(8,128)S(1)}, f32[512,256]{1,0:T(8,128)S(1)}, u32[]{:S(2)}, u32[]{:S(2)}) collective-permute-start(f32[512,256]{1,0:T(8,128)S(1)} %pad_maximum_fusion.1.refs_2_), channel_id=1, source_target_pairs={{0,8},{4,20},{8,0},{12,28},{16,24},{20,4},{24,16},{28,12},{1,9},{5... | collective-permute-start | bytes 1572872 | tf_op jit(solution)/shard_map/ppermute | solution.py:330
  72.3 7.0 %collective-permute-start.18 = (f32[512,256]{1,0:T(8,128)S(1)}, f32[512,256]{1,0:T(8,128)S(1)}, u32[]{:S(2)}, u32[]{:S(2)}) collective-permute-start(f32[512,256]{1,0:T(8,128)S(1)} %collective-permute-done.16.refs_1_), channel_id=1, source_target_pairs={{0,4},{4,0},{8,12},{12,8},{16,20},{20,16},{24,28},{28,24},{1,5},{5... | collective-permute-start | bytes 1572872 | tf_op jit(solution)/shard_map/ppermute | solution.py:325
  77.9 1.9 %collective-permute-start.19 = (f32[512,256]{1,0:T(8,128)S(1)}, f32[512,256]{1,0:T(8,128)S(1)}, u32[]{:S(2)}, u32[]{:S(2)}) collective-permute-start(f32[512,256]{1,0:T(8,128)S(1)} %collective-permute-done.14.refs_1_), channel_id=1, source_target_pairs={{0,4},{4,0},{8,12},{12,8},{16,20},{20,16},{24,28},{28,24},{1,5},{5... | collective-permute-start | bytes 1572872 | tf_op jit(solution)/shard_map/ppermute | solution.py:325

commit v3 on v2

--- a/solution.py
+++ b/solution.py
@@ -438,11 +438,12 @@
     late_back = flip(late_near, 1, size)
     early_far, residual = lax.optimization_barrier((early_far, residual))
     residual = subtract([nearer(1, 1), entry(0, 0)], [late_back, early_far], residual)
-    late_far, residual = lax.optimization_barrier((late_far, residual))
-    parts = [flip(early_far, 1, size), late_far, flip(late_far, 1, size)]
-    residual = subtract([entry(1, 0), entry(0, 1), entry(1, 1)], parts, residual)
-    summed = jnp.concatenate([after(early_sum, late_far), late_sum], 0)
+    summed = jnp.concatenate([after(early_sum, residual), late_sum], 0)
     top_rows = dot(summed, inverse, ((1,), (1,)), precise)
+    late_far, residual, top_rows = lax.optimization_barrier((late_far, residual, top_rows))
+    residual = subtract([entry(0, 1)], [late_far], residual)
+    parts = [flip(early_far, 1, size), flip(late_far, 1, size)]
+    residual = subtract([entry(1, 0), entry(1, 1)], parts, residual)
     return triangle, top_rows, residual
 
 

time: 85.2 us -> 85.2 us (level)
  waiting for transfers between devices: 14.9 us -> 13 us
  Pallas kernels: 43 us -> 44.6 us
    pallas_call x3 -> x4, Pallas kernels: 13.1 us -> 14.7 us  [residual_call(): pl.pallas_call(functools.partial(residual_kernel, firsts, each), in_specs...]
    ppermute x10, waiting for transfers between devices: 6.51 us -> 5.09 us  [exchange(): lax.ppermute(value, 'row', [(i, i ^ (bits[-1 - step] if i & 1 else bits[s...]
  transfers between devices with their start and end apart: 20 -> 20, of which waited for: 10 -> 9; matrix products, arithmetic and copies ran while one was open for 3% -> 3% of each run, Pallas kernels for 44% -> 47%
where the time goes in v3:
time: 85.2 us; the launch traced here: 84.3 us
  Pallas kernels  44.6 us (52%)
  starting transfers between devices  22.9 us (27%)
  waiting for transfers between devices  13 us (15%)
  matrix products  1.41 us (2%)
  other arithmetic  1.33 us (2%)
  between operations  1.07 us (1%)
    pallas_call x4, Pallas kernels, residual_call(): pl.pallas_call(functools.partial(residual_kernel, firsts, each), in_specs...  14.7 us
    ppermute x10, starting transfers between devices, exchange(): lax.ppermute(value, 'row', [(i, i ^ (bits[-1 - step] if i & 1 else bits[s...  13.3 us
    pallas_call x3, Pallas kernels, factor_call(): pl.pallas_call(body, out_shape=shapes, in_specs=in_specs, out_specs=[pl.B...  11.1 us
    pallas_call x4, Pallas kernels, cross_call(): pl.pallas_call(functools.partial(cross_kernel, first, each), in_specs=[pl...  10.2 us
    pallas_call x1, Pallas kernels, hold_call(): pl.pallas_call(hold_kernel, in_specs=[scalars, scalars, pl.BlockSpec(memo...  7.45 us
    ppermute x1, waiting for transfers between devices, gather_panel(): above = [lax.ppermute(shard, 'col', up)]  6.07 us
    ppermute x1, starting transfers between devices, gather_panel(): above = [lax.ppermute(shard, 'col', up)]  5.1 us
    ppermute x10, waiting for transfers between devices, exchange(): lax.ppermute(value, 'row', [(i, i ^ (bits[-1 - step] if i & 1 else bits[s...  5.09 us
  transfers between devices with their start and end apart: 20, of which 9 were waited for; matrix products, arithmetic and copies ran while one was open for 3% of the time, Pallas kernels for 47%

profile of v3, /device:TPU:0, one launch (start us, length us, event | category | flops | bytes accessed | tf_op | source)
XLA Modules:
  0.0 84.3 jit_solution(3105205186933320330)
XLA Ops:
  0.6 5.1 %collective-permute-start = (f32[64,1024]{1,0:T(8,128)}, f32[64,1024]{1,0:T(8,128)S(1)}, u32[]{:S(2)}, u32[]{:S(2)}) collective-permute-start(f32[64,1024]{1,0:T(8,128)} %refs_0_.1), channel_id=1, source_target_pairs={{0,3},{1,0},{2,1},{3,2},{4,7},{5,4},{6,5},{7,6},{8,11},{9,8},{10,9... | collective-permute-start | bytes 786440 | tf_op jit(solution)/shard_map/ppermute | solution.py:358
  5.7 6.1 %collective-permute-done.refs_1_ = f32[64,1024]{1,0:T(8,128)S(1)} collective-permute-done((f32[64,1024]{1,0:T(8,128)}, f32[64,1024]{1,0:T(8,128)S(1)}, u32[]{:S(2)}, u32[]{:S(2)}) %collective-permute-start) | collective-permute-done | bytes 262176 | tf_op jit(solution)/shard_map/ppermute | solution.py:358
  12.0 4.0 %collective-permute-start.1 = (f32[64,1024]{1,0:T(8,128)S(1)}, f32[64,1024]{1,0:T(8,128)S(1)}, u32[]{:S(2)}, u32[]{:S(2)}) collective-permute-start(f32[64,1024]{1,0:T(8,128)S(1)} %collective-permute-done.refs_1_), channel_id=1, source_target_pairs={{0,3},{1,0},{2,1},{3,2},{4,7},{5,4},{6,5},{7,6},{8,11},{9,8},{10,9... | collective-permute-start | bytes 786440 | tf_op jit(solution)/shard_map/ppermute | solution.py:363
  16.0 0.7 broadcast_add_fusion.1
  16.7 7.4 %hold.1 = (bf16[4096,1024]{1,0:T(8,128)(2,1)S(1)}, bf16[4096,1024]{1,0:T(8,128)(2,1)S(1)}) custom-call(s32[16]{0:T(128)S(1)} %pad_add_fusion.table_ref, s32[1]{0:T(128)} %bitcast.place_ref, f32[4096,1024]{1,0:T(8,128)} %window_ref.1), custom_call_target="tpu_custom_call" | custom-call | flops 1 | bytes 1 | tf_op jit(solution)/shard_map/hold/pallas_call | solution.py:96
  24.5 1.2 %gram.1 = (f32[256,1024]{1,0:T(8,128)S(1)}, bf16[1024,256]{1,0:T(8,128)(2,1)S(1)}, bf16[1024,256]{1,0:T(8,128)(2,1)S(1)}, f32[256,256]{1,0:T(8,128)S(1)}) custom-call(s32[1]{0:T(128)} %bitcast.place_ref, f32[64,1024]{1,0:T(8,128)S(1)} %copy-done, f32[64,1024]{1,0:T(8,128)S(1)} %collective-permute-done.refs_1_, ...), custom_call_target="tpu_custom_call" | custom-call | flops 99999997952 | bytes 1 | tf_op jit(solution)/shard_map/gram/pallas_call | solution.py:49
  25.7 1.6 %collective-permute-start.3 = (f32[256,256]{1,0:T(8,128)S(1)}, f32[256,256]{1,0:T(8,128)S(1)}, u32[]{:S(2)}, u32[]{:S(2)}) collective-permute-start(f32[256,256]{1,0:T(8,128)S(1)} %get-tuple-element.43), channel_id=1, source_target_pairs={{0,8},{4,20},{8,0},{12,28},{16,24},{20,4},{24,16},{28,12},{1,9},{5... | collective-permute-start | bytes 786440 | tf_op jit(solution)/shard_map/ppermute | solution.py:330
  27.3 2.5 %cross.4 = f32[1024,256]{1,0:T(8,128)S(1)} custom-call(s32[16]{0:T(128)S(1)} %pad_add_fusion.table_ref, bf16[4096,1024]{1,0:T(8,128)(2,1)S(1)} %get-tuple-element.40.window_high, bf16[4096,1024]{1,0:T(8,128)(2,1)S(1)} %get-tuple-element.45.window_low, bf16[1024,256]{1,0:T(8,128)(2,1)S(1)} %get-tuple-element.46.high_ref, ...), custom_call_target="tpu_custom_call" | custom-call | flops 1 | bytes 1 | tf_op jit(solution)/shard_map/cross/pallas_call | solution.py:133
  29.8 2.5 %cross.5 = f32[1024,256]{1,0:T(8,128)S(1)} custom-call(s32[16]{0:T(128)S(1)} %pad_add_fusion.table_ref, bf16[4096,1024]{1,0:T(8,128)(2,1)S(1)} %get-tuple-element.40.window_high, bf16[4096,1024]{1,0:T(8,128)(2,1)S(1)} %get-tuple-element.45.window_low, bf16[1024,256]{1,0:T(8,128)(2,1)S(1)} %get-tuple-element.46.high_ref, ...), custom_call_target="tpu_custom_call" | custom-call | flops 99999997952 | bytes 1 | tf_op jit(solution)/shard_map/cross/pallas_call | solution.py:133
  32.4 1.6 %collective-permute-start.4 = (f32[256,256]{1,0:T(8,128)S(1)}, f32[256,256]{1,0:T(8,128)S(1)}, u32[]{:S(2)}, u32[]{:S(2)}) collective-permute-start(f32[256,256]{1,0:T(8,128)S(1)} %add.53), channel_id=1, source_target_pairs={{0,16},{4,12},{8,24},{12,4},{16,0},{20,28},{24,8},{28,20},{1,17},{... | collective-permute-start | bytes 786440 | tf_op jit(solution)/shard_map/ppermute | solution.py:330
  34.1 1.3 %collective-permute-start.8 = (f32[512,256]{1,0:T(8,128)S(1)}, f32[512,256]{1,0:T(8,128)S(1)}, u32[]{:S(2)}, u32[]{:S(2)}) collective-permute-start(f32[512,256]{1,0:T(8,128)S(1)} %slice_add_fusion.1), channel_id=1, source_target_pairs={{0,8},{4,20},{8,0},{12,28},{16,24},{20,4},{24,16},{28,12},{1,9},{5... | collective-permute-start | bytes 1572872 | tf_op jit(solution)/shard_map/ppermute | solution.py:330
  35.4 2.5 %cross.6 = f32[1024,256]{1,0:T(8,128)S(1)} custom-call(s32[16]{0:T(128)S(1)} %pad_add_fusion.table_ref, bf16[4096,1024]{1,0:T(8,128)(2,1)S(1)} %get-tuple-element.40.window_high, bf16[4096,1024]{1,0:T(8,128)(2,1)S(1)} %get-tuple-element.45.window_low, bf16[1024,256]{1,0:T(8,128)(2,1)S(1)} %get-tuple-element.46.high_ref, ...), custom_call_target="tpu_custom_call" | custom-call | flops 1 | bytes 1 | tf_op jit(solution)/shard_map/cross/pallas_call | solution.py:133
  38.0 2.7 %cross.7 = f32[1024,256]{1,0:T(8,128)S(1)} custom-call(s32[16]{0:T(128)S(1)} %pad_add_fusion.table_ref, bf16[4096,1024]{1,0:T(8,128)(2,1)S(1)} %get-tuple-element.40.window_high, bf16[4096,1024]{1,0:T(8,128)(2,1)S(1)} %get-tuple-element.45.window_low, bf16[1024,256]{1,0:T(8,128)(2,1)S(1)} %get-tuple-element.46.high_ref, ...), custom_call_target="tpu_custom_call" | custom-call | flops 99999997952 | bytes 1 | tf_op jit(solution)/shard_map/cross/pallas_call | solution.py:133
  40.7 1.0 %collective-permute-done.4 = f32[256,256]{1,0:T(8,128)S(1)} collective-permute-done((f32[256,256]{1,0:T(8,128)S(1)}, f32[256,256]{1,0:T(8,128)S(1)}, u32[]{:S(2)}, u32[]{:S(2)}) %collective-permute-start.4) | collective-permute-done | bytes 262176 | tf_op jit(solution)/shard_map/ppermute | solution.py:330
  41.8 1.2 %collective-permute-start.9 = (f32[512,256]{1,0:T(8,128)S(1)}, f32[512,256]{1,0:T(8,128)S(1)}, u32[]{:S(2)}, u32[]{:S(2)}) collective-permute-start(f32[512,256]{1,0:T(8,128)S(1)} %slice_add_fusion), channel_id=1, source_target_pairs={{0,8},{4,20},{8,0},{12,28},{16,24},{20,4},{24,16},{28,12},{1,9},{5... | collective-permute-start | bytes 1572872 | tf_op jit(solution)/shard_map/ppermute | solution.py:330
  42.9 1.5 %collective-permute-done.6 = f32[256,256]{1,0:T(8,128)S(1)} collective-permute-done((f32[256,256]{1,0:T(8,128)S(1)}, f32[256,256]{1,0:T(8,128)S(1)}, u32[]{:S(2)}, u32[]{:S(2)}) %collective-permute-start.6) | collective-permute-done | bytes 262176 | tf_op jit(solution)/shard_map/ppermute | solution.py:325
  44.5 3.7 %factor.3 = (f32[256,256]{1,0:T(8,128)S(1)}, f32[256,128]{1,0:T(8,128)S(1)}) custom-call(f32[256,256]{1,0:T(8,128)S(1)} %add.56.refs_0_), custom_call_target="tpu_custom_call" | custom-call | flops 1 | bytes 1 | tf_op jit(solution)/shard_map/factor/pallas_call | solution.py:313
  48.3 1.6 %collective-permute-start.10 = (f32[256,256]{1,0:T(8,128)S(1)}, f32[256,256]{1,0:T(8,128)S(1)}, u32[]{:S(2)}, u32[]{:S(2)}) collective-permute-start(f32[256,256]{1,0:T(8,128)S(1)} %slice_add_fusion.8), channel_id=1, source_target_pairs={{0,16},{4,12},{8,24},{12,4},{16,0},{20,28},{24,8},{28,20},{1,17},{... | collective-permute-start | bytes 786440 | tf_op jit(solution)/shard_map/ppermute | solution.py:330
  49.9 1.1 %collective-permute-done.9 = f32[512,256]{1,0:T(8,128)S(1)} collective-permute-done((f32[512,256]{1,0:T(8,128)S(1)}, f32[512,256]{1,0:T(8,128)S(1)}, u32[]{:S(2)}, u32[]{:S(2)}) %collective-permute-start.9) | collective-permute-done | bytes 524320 | tf_op jit(solution)/shard_map/ppermute | solution.py:330
  51.1 1.6 %collective-permute-start.11 = (f32[256,256]{1,0:T(8,128)S(1)}, f32[256,256]{1,0:T(8,128)S(1)}, u32[]{:S(2)}, u32[]{:S(2)}) collective-permute-start(f32[256,256]{1,0:T(8,128)S(1)} %slice_add_fusion.6), channel_id=1, source_target_pairs={{0,16},{4,12},{8,24},{12,4},{16,0},{20,28},{24,8},{28,20},{1,17},{... | collective-permute-start | bytes 786440 | tf_op jit(solution)/shard_map/ppermute | solution.py:330
  52.7 3.7 %factor.4 = (f32[256,256]{1,0:T(8,128)S(1)}, f32[256,128]{1,0:T(8,128)S(1)}) custom-call(f32[256,256]{1,0:T(8,128)S(1)} %get-tuple-element.58.refs_0_, f32[256,128]{1,0:T(8,128)S(1)} %get-tuple-element.59.refs_1_), custom_call_target="tpu_custom_call" | custom-call | flops 1 | bytes 1 | tf_op jit(solution)/shard_map/factor/pallas_call | solution.py:313
  56.4 0.6 collective-permute-start.13
  57.6 1.6 %collective-permute-start.12 = (f32[256,256]{1,0:T(8,128)S(1)}, f32[256,256]{1,0:T(8,128)S(1)}, u32[]{:S(2)}, u32[]{:S(2)}) collective-permute-start(f32[256,256]{1,0:T(8,128)S(1)} %fusion.2), channel_id=1, source_target_pairs={{0,16},{4,12},{8,24},{12,4},{16,0},{20,28},{24,8},{28,20},{1,17},{... | collective-permute-start | bytes 786440 | tf_op jit(solution)/shard_map/ppermute | solution.py:330
  59.2 3.7 %factor.5 = (f32[256,256]{1,0:T(8,128)}, f32[256,128]{1,0:T(8,128)}, f32[256,256]{1,0:T(8,128)}, f32[256,256]{1,0:T(8,128)S(1)}, bf16[768,1024]{1,0:T(8,128)(2,1)S(1)}) custom-call(f32[256,256]{1,0:T(8,128)S(1)} %get-tuple-element.63.refs_0_, f32[256,128]{1,0:T(8,128)S(1)} %get-tuple-element.64.refs_1_, f32[256,1024]{1,0:T(8,128)S(1)} %get-tuple-element.65.refs_2_), custom_call_target="tpu_custom_call" | custom-call | flops 1 | bytes 1 | tf_op jit(solution)/shard_map/factor/pallas_call | solution.py:313
  63.0 1.2 %collective-permute-start.16 = (f32[512,256]{1,0:T(8,128)S(1)}, f32[512,256]{1,0:T(8,128)S(1)}, u32[]{:S(2)}, u32[]{:S(2)}) collective-permute-start(f32[512,256]{1,0:T(8,128)S(1)} %pad_maximum_fusion.3.refs_0_), channel_id=1, source_target_pairs={{0,8},{4,20},{8,0},{12,28},{16,24},{20,4},{24,16},{28,12},{1,9},{5... | collective-permute-start | bytes 1572872 | tf_op jit(solution)/shard_map/ppermute | solution.py:330
  64.2 1.5 %collective-permute-done.12 = f32[256,256]{1,0:T(8,128)S(1)} collective-permute-done((f32[256,256]{1,0:T(8,128)S(1)}, f32[256,256]{1,0:T(8,128)S(1)}, u32[]{:S(2)}, u32[]{:S(2)}) %collective-permute-start.12) | collective-permute-done | bytes 262176 | tf_op jit(solution)/shard_map/ppermute | solution.py:330
  65.8 1.2 %collective-permute-start.14 = (f32[512,256]{1,0:T(8,128)S(1)}, f32[512,256]{1,0:T(8,128)S(1)}, u32[]{:S(2)}, u32[]{:S(2)}) collective-permute-start(f32[512,256]{1,0:T(8,128)S(1)} %pad_maximum_fusion.1.refs_2_), channel_id=1, source_target_pairs={{0,8},{4,20},{8,0},{12,28},{16,24},{20,4},{24,16},{28,12},{1,9},{5... | collective-permute-start | bytes 1572872 | tf_op jit(solution)/shard_map/ppermute | solution.py:330
  67.0 4.9 %residual.4.refs_2_ = f32[4096,1024]{1,0:T(8,128)} custom-call(s32[16]{0:T(128)S(1)} %pad_add_fusion.table_ref, bf16[4096,1024]{1,0:T(8,128)(2,1)S(1)} %get-tuple-element.40.window_high, bf16[4096,1024]{1,0:T(8,128)(2,1)S(1)} %get-tuple-element.45.window_low, bf16[768,1024]{1,0:T(8,128)(2,1)S(1)} %get-tuple-element.67.weight_ref, ...), custom_call_target="tpu_custom_call" | custom-call | flops 1 | bytes 1 | tf_op jit(solution)/shard_map/residual/pallas_call | solution.py:185
  72.3 3.6 %residual.5.refs_1_ = f32[4096,1024]{1,0:T(8,128)} custom-call(s32[16]{0:T(128)S(1)} %pad_add_fusion.table_ref, bf16[4096,1024]{1,0:T(8,128)(2,1)S(1)} %get-tuple-element.40.window_high, bf16[4096,1024]{1,0:T(8,128)(2,1)S(1)} %get-tuple-element.45.window_low, bf16[768,1024]{1,0:T(8,128)(2,1)S(1)} %get-tuple-element.67.weight_ref, ...), custom_call_target="tpu_custom_call", output_to_operand_aliasing={{}: (6, {})} | custom-call | flops 1 | bytes 1 | tf_op jit(solution)/shard_map/residual/pallas_call | solution.py:185
  75.9 1.4 %fusion = f32[512,256]{1,0:T(8,128)} fusion(f32[256,256]{1,0:T(8,128)S(1)} %get-tuple-element.73, f32[256,256]{1,0:T(8,128)S(1)} %fusion.2, f32[256,256]{1,0:T(8,128)S(1)} %fusion.3), kind=kOutput, calls=%fused_computation.2 | convolution fusion | flops 402784256 | bytes 1310720 | tf_op jit(solution)/shard_map/dot_general | solution.py:20
  77.9 2.6 %residual.6.refs_2_ = f32[4096,1024]{1,0:T(8,128)} custom-call(s32[16]{0:T(128)S(1)} %pad_add_fusion.table_ref, bf16[4096,1024]{1,0:T(8,128)(2,1)S(1)} %get-tuple-element.40.window_high, bf16[4096,1024]{1,0:T(8,128)(2,1)S(1)} %get-tuple-element.45.window_low, bf16[768,1024]{1,0:T(8,128)(2,1)S(1)} %get-tuple-element.67.weight_ref, ...), custom_call_target="tpu_custom_call", output_to_operand_aliasing={{}: (5, {})} | custom-call | flops 1 | bytes 1 | tf_op jit(solution)/shard_map/residual/pallas_call | solution.py:185
  80.5 3.6 %residual.7 = f32[4096,1024]{1,0:T(8,128)} custom-call(s32[16]{0:T(128)S(1)} %pad_add_fusion.table_ref, bf16[4096,1024]{1,0:T(8,128)(2,1)S(1)} %get-tuple-element.40.window_high, bf16[4096,1024]{1,0:T(8,128)(2,1)S(1)} %get-tuple-element.45.window_low, bf16[768,1024]{1,0:T(8,128)(2,1)S(1)} %get-tuple-element.67.weight_ref, ...), custom_call_target="tpu_custom_call", output_to_operand_aliasing={{}: (6, {})} | custom-call | flops 1 | bytes 1 | tf_op jit(solution)/shard_map/residual/pallas_call | solution.py:185
  (37 shorter events, 2.9 us)
Async XLA Ops:
  0.6 23.9 %copy-start = (f32[64,1024]{1,0:T(8,128)S(1)}, f32[64,1024]{1,0:T(8,128)}, u32[]{:S(2)}) copy-start(f32[64,1024]{1,0:T(8,128)} %refs_0_.1) | copy-start | bytes 786436
  0.6 11.2 %collective-permute-start = (f32[64,1024]{1,0:T(8,128)}, f32[64,1024]{1,0:T(8,128)S(1)}, u32[]{:S(2)}, u32[]{:S(2)}) collective-permute-start(f32[64,1024]{1,0:T(8,128)} %refs_0_.1), channel_id=1, source_target_pairs={{0,3},{1,0},{2,1},{3,2},{4,7},{5,4},{6,5},{7,6},{8,11},{9,8},{10,9... | collective-permute-start | bytes 786440 | tf_op jit(solution)/shard_map/ppermute | solution.py:358
  11.8 12.4 %collective-permute-start.2 = (f32[64,1024]{1,0:T(8,128)}, f32[64,1024]{1,0:T(8,128)S(1)}, u32[]{:S(2)}, u32[]{:S(2)}) collective-permute-start(f32[64,1024]{1,0:T(8,128)} %refs_0_.1), channel_id=1, source_target_pairs={{0,1},{1,2},{2,3},{3,0},{4,5},{5,6},{6,7},{7,4},{8,9},{9,10},{10,1... | collective-permute-start | bytes 786440 | tf_op jit(solution)/shard_map/ppermute | solution.py:365
  12.0 12.5 %collective-permute-start.1 = (f32[64,1024]{1,0:T(8,128)S(1)}, f32[64,1024]{1,0:T(8,128)S(1)}, u32[]{:S(2)}, u32[]{:S(2)}) collective-permute-start(f32[64,1024]{1,0:T(8,128)S(1)} %collective-permute-done.refs_1_), channel_id=1, source_target_pairs={{0,3},{1,0},{2,1},{3,2},{4,7},{5,4},{6,5},{7,6},{8,11},{9,8},{10,9... | collective-permute-start | bytes 786440 | tf_op jit(solution)/shard_map/ppermute | solution.py:363
  25.7 6.7 %collective-permute-start.3 = (f32[256,256]{1,0:T(8,128)S(1)}, f32[256,256]{1,0:T(8,128)S(1)}, u32[]{:S(2)}, u32[]{:S(2)}) collective-permute-start(f32[256,256]{1,0:T(8,128)S(1)} %get-tuple-element.43), channel_id=1, source_target_pairs={{0,8},{4,20},{8,0},{12,28},{16,24},{20,4},{24,16},{28,12},{1,9},{5... | collective-permute-start | bytes 786440 | tf_op jit(solution)/shard_map/ppermute | solution.py:330
  29.8 4.2 %collective-permute-start.5 = (f32[1024,256]{1,0:T(8,128)S(1)}, f32[1024,256]{1,0:T(8,128)S(1)}, u32[]{:S(2)}, u32[]{:S(2)}) collective-permute-start(f32[1024,256]{1,0:T(8,128)S(1)} %cross.4), channel_id=1, source_target_pairs={{0,4},{4,0},{8,12},{12,8},{16,20},{20,16},{24,28},{28,24},{1,5},{5... | collective-permute-start | bytes 3145736 | tf_op jit(solution)/shard_map/ppermute | solution.py:325
  32.4 9.2 %collective-permute-start.4 = (f32[256,256]{1,0:T(8,128)S(1)}, f32[256,256]{1,0:T(8,128)S(1)}, u32[]{:S(2)}, u32[]{:S(2)}) collective-permute-start(f32[256,256]{1,0:T(8,128)S(1)} %add.53), channel_id=1, source_target_pairs={{0,16},{4,12},{8,24},{12,4},{16,0},{20,28},{24,8},{28,20},{1,17},{... | collective-permute-start | bytes 786440 | tf_op jit(solution)/shard_map/ppermute | solution.py:330
  34.1 14.2 %collective-permute-start.8 = (f32[512,256]{1,0:T(8,128)S(1)}, f32[512,256]{1,0:T(8,128)S(1)}, u32[]{:S(2)}, u32[]{:S(2)}) collective-permute-start(f32[512,256]{1,0:T(8,128)S(1)} %slice_add_fusion.1), channel_id=1, source_target_pairs={{0,8},{4,20},{8,0},{12,28},{16,24},{20,4},{24,16},{28,12},{1,9},{5... | collective-permute-start | bytes 1572872 | tf_op jit(solution)/shard_map/ppermute | solution.py:330
  37.9 3.8 %collective-permute-start.7 = (f32[1024,256]{1,0:T(8,128)S(1)}, f32[1024,256]{1,0:T(8,128)S(1)}, u32[]{:S(2)}, u32[]{:S(2)}) collective-permute-start(f32[1024,256]{1,0:T(8,128)S(1)} %cross.6), channel_id=1, source_target_pairs={{0,4},{4,0},{8,12},{12,8},{16,20},{20,16},{24,28},{28,24},{1,5},{5... | collective-permute-start | bytes 3145736 | tf_op jit(solution)/shard_map/ppermute | solution.py:325
  41.8 9.2 %collective-permute-start.9 = (f32[512,256]{1,0:T(8,128)S(1)}, f32[512,256]{1,0:T(8,128)S(1)}, u32[]{:S(2)}, u32[]{:S(2)}) collective-permute-start(f32[512,256]{1,0:T(8,128)S(1)} %slice_add_fusion), channel_id=1, source_target_pairs={{0,8},{4,20},{8,0},{12,28},{16,24},{20,4},{24,16},{28,12},{1,9},{5... | collective-permute-start | bytes 1572872 | tf_op jit(solution)/shard_map/ppermute | solution.py:330
  42.9 1.5 %collective-permute-start.6 = (f32[256,256]{1,0:T(8,128)S(1)}, f32[256,256]{1,0:T(8,128)S(1)}, u32[]{:S(2)}, u32[]{:S(2)}) collective-permute-start(f32[256,256]{1,0:T(8,128)S(1)} %add.55), channel_id=1, source_target_pairs={{0,4},{4,0},{8,12},{12,8},{16,20},{20,16},{24,28},{28,24},{1,5},{5... | collective-permute-start | bytes 786440 | tf_op jit(solution)/shard_map/ppermute | solution.py:325
  48.3 8.1 %collective-permute-start.10 = (f32[256,256]{1,0:T(8,128)S(1)}, f32[256,256]{1,0:T(8,128)S(1)}, u32[]{:S(2)}, u32[]{:S(2)}) collective-permute-start(f32[256,256]{1,0:T(8,128)S(1)} %slice_add_fusion.8), channel_id=1, source_target_pairs={{0,16},{4,12},{8,24},{12,4},{16,0},{20,28},{24,8},{28,20},{1,17},{... | collective-permute-start | bytes 786440 | tf_op jit(solution)/shard_map/ppermute | solution.py:330
  51.1 6.5 %collective-permute-start.11 = (f32[256,256]{1,0:T(8,128)S(1)}, f32[256,256]{1,0:T(8,128)S(1)}, u32[]{:S(2)}, u32[]{:S(2)}) collective-permute-start(f32[256,256]{1,0:T(8,128)S(1)} %slice_add_fusion.6), channel_id=1, source_target_pairs={{0,16},{4,12},{8,24},{12,4},{16,0},{20,28},{24,8},{28,20},{1,17},{... | collective-permute-start | bytes 786440 | tf_op jit(solution)/shard_map/ppermute | solution.py:330
  56.4 6.5 %collective-permute-start.13 = (f32[256,256]{1,0:T(8,128)S(1)}, f32[256,256]{1,0:T(8,128)S(1)}, u32[]{:S(2)}, u32[]{:S(2)}) collective-permute-start(f32[256,256]{1,0:T(8,128)S(1)} %fusion.3), channel_id=1, source_target_pairs={{0,16},{4,12},{8,24},{12,4},{16,0},{20,28},{24,8},{28,20},{1,17},{... | collective-permute-start | bytes 786440 | tf_op jit(solution)/shard_map/ppermute | solution.py:330
  57.6 8.1 %collective-permute-start.12 = (f32[256,256]{1,0:T(8,128)S(1)}, f32[256,256]{1,0:T(8,128)S(1)}, u32[]{:S(2)}, u32[]{:S(2)}) collective-permute-start(f32[256,256]{1,0:T(8,128)S(1)} %fusion.2), channel_id=1, source_target_pairs={{0,16},{4,12},{8,24},{12,4},{16,0},{20,28},{24,8},{28,20},{1,17},{... | collective-permute-start | bytes 786440 | tf_op jit(solution)/shard_map/ppermute | solution.py:330
  63.0 4.1 %collective-permute-start.17 = (f32[512,256]{1,0:T(8,128)S(1)}, f32[512,256]{1,0:T(8,128)S(1)}, u32[]{:S(2)}, u32[]{:S(2)}) collective-permute-start(f32[512,256]{1,0:T(8,128)S(1)} %pad_maximum_fusion.3.refs_0_), channel_id=1, source_target_pairs={{0,4},{4,0},{8,12},{12,8},{16,20},{20,16},{24,28},{28,24},{1,5},{5... | collective-permute-start | bytes 1572872 | tf_op jit(solution)/shard_map/ppermute | solution.py:325
  63.0 9.2 %collective-permute-start.16 = (f32[512,256]{1,0:T(8,128)S(1)}, f32[512,256]{1,0:T(8,128)S(1)}, u32[]{:S(2)}, u32[]{:S(2)}) collective-permute-start(f32[512,256]{1,0:T(8,128)S(1)} %pad_maximum_fusion.3.refs_0_), channel_id=1, source_target_pairs={{0,8},{4,20},{8,0},{12,28},{16,24},{20,4},{24,16},{28,12},{1,9},{5... | collective-permute-start | bytes 1572872 | tf_op jit(solution)/shard_map/ppermute | solution.py:330
  65.7 6.6 %collective-permute-start.15 = (f32[512,256]{1,0:T(8,128)S(1)}, f32[512,256]{1,0:T(8,128)S(1)}, u32[]{:S(2)}, u32[]{:S(2)}) collective-permute-start(f32[512,256]{1,0:T(8,128)S(1)} %pad_maximum_fusion.1.refs_2_), channel_id=1, source_target_pairs={{0,4},{4,0},{8,12},{12,8},{16,20},{20,16},{24,28},{28,24},{1,5},{5... | collective-permute-start | bytes 1572872 | tf_op jit(solution)/shard_map/ppermute | solution.py:325
  65.8 12.1 %collective-permute-start.14 = (f32[512,256]{1,0:T(8,128)S(1)}, f32[512,256]{1,0:T(8,128)S(1)}, u32[]{:S(2)}, u32[]{:S(2)}) collective-permute-start(f32[512,256]{1,0:T(8,128)S(1)} %pad_maximum_fusion.1.refs_2_), channel_id=1, source_target_pairs={{0,8},{4,20},{8,0},{12,28},{16,24},{20,4},{24,16},{28,12},{1,9},{5... | collective-permute-start | bytes 1572872 | tf_op jit(solution)/shard_map/ppermute | solution.py:330
  72.3 8.2 %collective-permute-start.18 = (f32[512,256]{1,0:T(8,128)S(1)}, f32[512,256]{1,0:T(8,128)S(1)}, u32[]{:S(2)}, u32[]{:S(2)}) collective-permute-start(f32[512,256]{1,0:T(8,128)S(1)} %collective-permute-done.16.refs_1_), channel_id=1, source_target_pairs={{0,4},{4,0},{8,12},{12,8},{16,20},{20,16},{24,28},{28,24},{1,5},{5... | collective-permute-start | bytes 1572872 | tf_op jit(solution)/shard_map/ppermute | solution.py:325
  77.9 2.6 %collective-permute-start.19 = (f32[512,256]{1,0:T(8,128)S(1)}, f32[512,256]{1,0:T(8,128)S(1)}, u32[]{:S(2)}, u32[]{:S(2)}) collective-permute-start(f32[512,256]{1,0:T(8,128)S(1)} %collective-permute-done.14.refs_0_), channel_id=1, source_target_pairs={{0,4},{4,0},{8,12},{12,8},{16,20},{20,16},{24,28},{28,24},{1,5},{5... | collective-permute-start | bytes 1572872 | tf_op jit(solution)/shard_map/ppermute | solution.py:325

commit v4 on v3

--- a/solution.py
+++ b/solution.py
@@ -407,11 +407,11 @@
     gram = after(gram, kept)
     (given,) = products(1, 1, 1, BRIEF, early_sum, gram)
     arrived = flip(given, 1, size)
+    (kept,) = products(0, 1, 1, LONG, given)
+    late = sum_shares(kept, arrived, bits)
+    late_sum = next(late)
     for step in range(1, steps):
-        gram = gram + after(exchange(gram, step, bits), given)
-    (kept,) = products(0, 1, 1, LONG, given)
-    late = sum_shares(after(kept, gram), arrived, bits)
-    late_sum = next(late)
+        gram = gram + after(exchange(gram, step, bits), late_sum)
     gram = gram + flip(gram, 1, size)
 
     blocks = whole.shape[0] // BLOCK

time: 85.2 us -> 84.1 us (0.987)
  starting transfers between devices: 22.9 us -> 21.9 us
    ppermute x10, starting transfers between devices: 13.3 us -> 12.2 us  [exchange(): lax.ppermute(value, 'row', [(i, i ^ (bits[-1 - step] if i & 1 else bits[s...]
  transfers between devices with their start and end apart: 20 -> 20, of which waited for: 9 -> 9; matrix products, arithmetic and copies ran while one was open for 3% -> 3% of each run, Pallas kernels for 47% -> 48%
where the time goes in v4:
time: 84.1 us; the launch traced here: 83.1 us
  Pallas kernels  44.6 us (53%)
  starting transfers between devices  21.9 us (26%)
  waiting for transfers between devices  12.8 us (15%)
  matrix products  1.41 us (2%)
  other arithmetic  1.32 us (2%)
  between operations  1.08 us (1%)
    pallas_call x4, Pallas kernels, residual_call(): pl.pallas_call(functools.partial(residual_kernel, firsts, each), in_specs...  14.7 us
    ppermute x10, starting transfers between devices, exchange(): lax.ppermute(value, 'row', [(i, i ^ (bits[-1 - step] if i & 1 else bits[s...  12.2 us
    pallas_call x3, Pallas kernels, factor_call(): pl.pallas_call(body, out_shape=shapes, in_specs=in_specs, out_specs=[pl.B...  11.1 us
    pallas_call x4, Pallas kernels, cross_call(): pl.pallas_call(functools.partial(cross_kernel, first, each), in_specs=[pl...  10.2 us
    pallas_call x1, Pallas kernels, hold_call(): pl.pallas_call(hold_kernel, in_specs=[scalars, scalars, pl.BlockSpec(memo...  7.45 us
    ppermute x1, waiting for transfers between devices, gather_panel(): above = [lax.ppermute(shard, 'col', up)]  6.07 us
    ppermute x1, starting transfers between devices, gather_panel(): above = [lax.ppermute(shard, 'col', up)]  5.1 us
    ppermute x10, waiting for transfers between devices, exchange(): lax.ppermute(value, 'row', [(i, i ^ (bits[-1 - step] if i & 1 else bits[s...  4.96 us
  transfers between devices with their start and end apart: 20, of which 9 were waited for; matrix products, arithmetic and copies ran while one was open for 3% of the time, Pallas kernels for 48%

profile of v4, /device:TPU:0, one launch (start us, length us, event | category | flops | bytes accessed | tf_op | source)
XLA Modules:
  0.0 83.1 jit_solution(145143674290288109)
XLA Ops:
  0.6 5.1 %collective-permute-start = (f32[64,1024]{1,0:T(8,128)}, f32[64,1024]{1,0:T(8,128)S(1)}, u32[]{:S(2)}, u32[]{:S(2)}) collective-permute-start(f32[64,1024]{1,0:T(8,128)} %refs_0_.1), channel_id=1, source_target_pairs={{0,3},{1,0},{2,1},{3,2},{4,7},{5,4},{6,5},{7,6},{8,11},{9,8},{10,9... | collective-permute-start | bytes 786440 | tf_op jit(solution)/shard_map/ppermute | solution.py:358
  5.7 6.1 %collective-permute-done.refs_1_ = f32[64,1024]{1,0:T(8,128)S(1)} collective-permute-done((f32[64,1024]{1,0:T(8,128)}, f32[64,1024]{1,0:T(8,128)S(1)}, u32[]{:S(2)}, u32[]{:S(2)}) %collective-permute-start) | collective-permute-done | bytes 262176 | tf_op jit(solution)/shard_map/ppermute | solution.py:358
  12.0 4.0 %collective-permute-start.1 = (f32[64,1024]{1,0:T(8,128)S(1)}, f32[64,1024]{1,0:T(8,128)S(1)}, u32[]{:S(2)}, u32[]{:S(2)}) collective-permute-start(f32[64,1024]{1,0:T(8,128)S(1)} %collective-permute-done.refs_1_), channel_id=1, source_target_pairs={{0,3},{1,0},{2,1},{3,2},{4,7},{5,4},{6,5},{7,6},{8,11},{9,8},{10,9... | collective-permute-start | bytes 786440 | tf_op jit(solution)/shard_map/ppermute | solution.py:363
  16.0 0.7 broadcast_add_fusion.1
  16.7 7.4 %hold.1 = (bf16[4096,1024]{1,0:T(8,128)(2,1)S(1)}, bf16[4096,1024]{1,0:T(8,128)(2,1)S(1)}) custom-call(s32[16]{0:T(128)S(1)} %pad_add_fusion.table_ref, s32[1]{0:T(128)} %bitcast.place_ref, f32[4096,1024]{1,0:T(8,128)} %window_ref.1), custom_call_target="tpu_custom_call" | custom-call | flops 1 | bytes 1 | tf_op jit(solution)/shard_map/hold/pallas_call | solution.py:96
  24.5 1.2 %gram.1 = (f32[256,1024]{1,0:T(8,128)S(1)}, bf16[1024,256]{1,0:T(8,128)(2,1)S(1)}, bf16[1024,256]{1,0:T(8,128)(2,1)S(1)}, f32[256,256]{1,0:T(8,128)S(1)}) custom-call(s32[1]{0:T(128)} %bitcast.place_ref, f32[64,1024]{1,0:T(8,128)S(1)} %copy-done, f32[64,1024]{1,0:T(8,128)S(1)} %collective-permute-done.refs_1_, ...), custom_call_target="tpu_custom_call" | custom-call | flops 99999997952 | bytes 1 | tf_op jit(solution)/shard_map/gram/pallas_call | solution.py:49
  25.7 1.6 %collective-permute-start.3 = (f32[256,256]{1,0:T(8,128)S(1)}, f32[256,256]{1,0:T(8,128)S(1)}, u32[]{:S(2)}, u32[]{:S(2)}) collective-permute-start(f32[256,256]{1,0:T(8,128)S(1)} %get-tuple-element.42), channel_id=1, source_target_pairs={{0,8},{4,20},{8,0},{12,28},{16,24},{20,4},{24,16},{28,12},{1,9},{5... | collective-permute-start | bytes 786440 | tf_op jit(solution)/shard_map/ppermute | solution.py:330
  27.3 2.5 %cross.4 = f32[1024,256]{1,0:T(8,128)S(1)} custom-call(s32[16]{0:T(128)S(1)} %pad_add_fusion.table_ref, bf16[4096,1024]{1,0:T(8,128)(2,1)S(1)} %get-tuple-element.39.window_high, bf16[4096,1024]{1,0:T(8,128)(2,1)S(1)} %get-tuple-element.44.window_low, bf16[1024,256]{1,0:T(8,128)(2,1)S(1)} %get-tuple-element.45.high_ref, ...), custom_call_target="tpu_custom_call" | custom-call | flops 1 | bytes 1 | tf_op jit(solution)/shard_map/cross/pallas_call | solution.py:133
  29.8 2.5 %cross.5 = f32[1024,256]{1,0:T(8,128)S(1)} custom-call(s32[16]{0:T(128)S(1)} %pad_add_fusion.table_ref, bf16[4096,1024]{1,0:T(8,128)(2,1)S(1)} %get-tuple-element.39.window_high, bf16[4096,1024]{1,0:T(8,128)(2,1)S(1)} %get-tuple-element.44.window_low, bf16[1024,256]{1,0:T(8,128)(2,1)S(1)} %get-tuple-element.45.high_ref, ...), custom_call_target="tpu_custom_call" | custom-call | flops 99999997952 | bytes 1 | tf_op jit(solution)/shard_map/cross/pallas_call | solution.py:133
  32.4 1.6 %collective-permute-start.4 = (f32[256,256]{1,0:T(8,128)S(1)}, f32[256,256]{1,0:T(8,128)S(1)}, u32[]{:S(2)}, u32[]{:S(2)}) collective-permute-start(f32[256,256]{1,0:T(8,128)S(1)} %add.53), channel_id=1, source_target_pairs={{0,16},{4,12},{8,24},{12,4},{16,0},{20,28},{24,8},{28,20},{1,17},{... | collective-permute-start | bytes 786440 | tf_op jit(solution)/shard_map/ppermute | solution.py:330
  34.1 1.3 %collective-permute-start.8 = (f32[512,256]{1,0:T(8,128)S(1)}, f32[512,256]{1,0:T(8,128)S(1)}, u32[]{:S(2)}, u32[]{:S(2)}) collective-permute-start(f32[512,256]{1,0:T(8,128)S(1)} %slice_add_fusion.1), channel_id=1, source_target_pairs={{0,8},{4,20},{8,0},{12,28},{16,24},{20,4},{24,16},{28,12},{1,9},{5... | collective-permute-start | bytes 1572872 | tf_op jit(solution)/shard_map/ppermute | solution.py:330
  35.4 2.5 %cross.6 = f32[1024,256]{1,0:T(8,128)S(1)} custom-call(s32[16]{0:T(128)S(1)} %pad_add_fusion.table_ref, bf16[4096,1024]{1,0:T(8,128)(2,1)S(1)} %get-tuple-element.39.window_high, bf16[4096,1024]{1,0:T(8,128)(2,1)S(1)} %get-tuple-element.44.window_low, bf16[1024,256]{1,0:T(8,128)(2,1)S(1)} %get-tuple-element.45.high_ref, ...), custom_call_target="tpu_custom_call" | custom-call | flops 1 | bytes 1 | tf_op jit(solution)/shard_map/cross/pallas_call | solution.py:133
  38.0 2.7 %cross.7 = f32[1024,256]{1,0:T(8,128)S(1)} custom-call(s32[16]{0:T(128)S(1)} %pad_add_fusion.table_ref, bf16[4096,1024]{1,0:T(8,128)(2,1)S(1)} %get-tuple-element.39.window_high, bf16[4096,1024]{1,0:T(8,128)(2,1)S(1)} %get-tuple-element.44.window_low, bf16[1024,256]{1,0:T(8,128)(2,1)S(1)} %get-tuple-element.45.high_ref, ...), custom_call_target="tpu_custom_call" | custom-call | flops 99999997952 | bytes 1 | tf_op jit(solution)/shard_map/cross/pallas_call | solution.py:133
  40.8 0.8 collective-permute-start.9
  41.8 1.5 %collective-permute-done.7 = f32[256,256]{1,0:T(8,128)S(1)} collective-permute-done((f32[256,256]{1,0:T(8,128)S(1)}, f32[256,256]{1,0:T(8,128)S(1)}, u32[]{:S(2)}, u32[]{:S(2)}) %collective-permute-start.7) | collective-permute-done | bytes 262176 | tf_op jit(solution)/shard_map/ppermute | solution.py:325
  43.3 3.7 %factor.3 = (f32[256,256]{1,0:T(8,128)S(1)}, f32[256,128]{1,0:T(8,128)S(1)}) custom-call(f32[256,256]{1,0:T(8,128)S(1)} %add.57.refs_0_), custom_call_target="tpu_custom_call" | custom-call | flops 1 | bytes 1 | tf_op jit(solution)/shard_map/factor/pallas_call | solution.py:313
  47.1 1.6 %collective-permute-start.10 = (f32[256,256]{1,0:T(8,128)S(1)}, f32[256,256]{1,0:T(8,128)S(1)}, u32[]{:S(2)}, u32[]{:S(2)}) collective-permute-start(f32[256,256]{1,0:T(8,128)S(1)} %slice_add_fusion.8), channel_id=1, source_target_pairs={{0,16},{4,12},{8,24},{12,4},{16,0},{20,28},{24,8},{28,20},{1,17},{... | collective-permute-start | bytes 786440 | tf_op jit(solution)/shard_map/ppermute | solution.py:330
  48.7 1.3 %collective-permute-done.9 = f32[512,256]{1,0:T(8,128)S(1)} collective-permute-done((f32[512,256]{1,0:T(8,128)S(1)}, f32[512,256]{1,0:T(8,128)S(1)}, u32[]{:S(2)}, u32[]{:S(2)}) %collective-permute-start.9) | collective-permute-done | bytes 524320 | tf_op jit(solution)/shard_map/ppermute | solution.py:330
  50.1 1.2 %collective-permute-start.11 = (f32[256,256]{1,0:T(8,128)S(1)}, f32[256,256]{1,0:T(8,128)S(1)}, u32[]{:S(2)}, u32[]{:S(2)}) collective-permute-start(f32[256,256]{1,0:T(8,128)S(1)} %slice_add_fusion.6), channel_id=1, source_target_pairs={{0,16},{4,12},{8,24},{12,4},{16,0},{20,28},{24,8},{28,20},{1,17},{... | collective-permute-start | bytes 786440 | tf_op jit(solution)/shard_map/ppermute | solution.py:330
  51.2 3.7 %factor.4 = (f32[256,256]{1,0:T(8,128)S(1)}, f32[256,128]{1,0:T(8,128)S(1)}) custom-call(f32[256,256]{1,0:T(8,128)S(1)} %get-tuple-element.56.refs_0_, f32[256,128]{1,0:T(8,128)S(1)} %get-tuple-element.57.refs_1_), custom_call_target="tpu_custom_call" | custom-call | flops 1 | bytes 1 | tf_op jit(solution)/shard_map/factor/pallas_call | solution.py:313
  55.0 1.0 %collective-permute-start.13 = (f32[256,256]{1,0:T(8,128)S(1)}, f32[256,256]{1,0:T(8,128)S(1)}, u32[]{:S(2)}, u32[]{:S(2)}) collective-permute-start(f32[256,256]{1,0:T(8,128)S(1)} %fusion.3), channel_id=1, source_target_pairs={{0,16},{4,12},{8,24},{12,4},{16,0},{20,28},{24,8},{28,20},{1,17},{... | collective-permute-start | bytes 786440 | tf_op jit(solution)/shard_map/ppermute | solution.py:330
  56.6 1.4 %collective-permute-start.12 = (f32[256,256]{1,0:T(8,128)S(1)}, f32[256,256]{1,0:T(8,128)S(1)}, u32[]{:S(2)}, u32[]{:S(2)}) collective-permute-start(f32[256,256]{1,0:T(8,128)S(1)} %fusion.2), channel_id=1, source_target_pairs={{0,16},{4,12},{8,24},{12,4},{16,0},{20,28},{24,8},{28,20},{1,17},{... | collective-permute-start | bytes 786440 | tf_op jit(solution)/shard_map/ppermute | solution.py:330
  58.0 3.7 %factor.5 = (f32[256,256]{1,0:T(8,128)}, f32[256,128]{1,0:T(8,128)}, f32[256,256]{1,0:T(8,128)}, f32[256,256]{1,0:T(8,128)S(1)}, bf16[768,1024]{1,0:T(8,128)(2,1)S(1)}) custom-call(f32[256,256]{1,0:T(8,128)S(1)} %get-tuple-element.61.refs_0_, f32[256,128]{1,0:T(8,128)S(1)} %get-tuple-element.62.refs_1_, f32[256,1024]{1,0:T(8,128)S(1)} %get-tuple-element.63.refs_2_), custom_call_target="tpu_custom_call" | custom-call | flops 1 | bytes 1 | tf_op jit(solution)/shard_map/factor/pallas_call | solution.py:313
  61.8 1.2 %collective-permute-start.16 = (f32[512,256]{1,0:T(8,128)S(1)}, f32[512,256]{1,0:T(8,128)S(1)}, u32[]{:S(2)}, u32[]{:S(2)}) collective-permute-start(f32[512,256]{1,0:T(8,128)S(1)} %pad_maximum_fusion.3.refs_0_), channel_id=1, source_target_pairs={{0,8},{4,20},{8,0},{12,28},{16,24},{20,4},{24,16},{28,12},{1,9},{5... | collective-permute-start | bytes 1572872 | tf_op jit(solution)/shard_map/ppermute | solution.py:330
  63.0 1.3 %collective-permute-done.12 = f32[256,256]{1,0:T(8,128)S(1)} collective-permute-done((f32[256,256]{1,0:T(8,128)S(1)}, f32[256,256]{1,0:T(8,128)S(1)}, u32[]{:S(2)}, u32[]{:S(2)}) %collective-permute-start.12) | collective-permute-done | bytes 262176 | tf_op jit(solution)/shard_map/ppermute | solution.py:330
  64.4 0.6 collective-permute-start.14
  65.0 4.9 %residual.4.refs_2_ = f32[4096,1024]{1,0:T(8,128)} custom-call(s32[16]{0:T(128)S(1)} %pad_add_fusion.table_ref, bf16[4096,1024]{1,0:T(8,128)(2,1)S(1)} %get-tuple-element.39.window_high, bf16[4096,1024]{1,0:T(8,128)(2,1)S(1)} %get-tuple-element.44.window_low, bf16[768,1024]{1,0:T(8,128)(2,1)S(1)} %get-tuple-element.65.weight_ref, ...), custom_call_target="tpu_custom_call" | custom-call | flops 1 | bytes 1 | tf_op jit(solution)/shard_map/residual/pallas_call | solution.py:185
  69.9 1.2 %collective-permute-done.16.refs_1_ = f32[512,256]{1,0:T(8,128)S(1)} collective-permute-done((f32[512,256]{1,0:T(8,128)S(1)}, f32[512,256]{1,0:T(8,128)S(1)}, u32[]{:S(2)}, u32[]{:S(2)}) %collective-permute-start.16) | collective-permute-done | bytes 524320 | tf_op jit(solution)/shard_map/ppermute | solution.py:330
  71.1 3.6 %residual.5.refs_1_ = f32[4096,1024]{1,0:T(8,128)} custom-call(s32[16]{0:T(128)S(1)} %pad_add_fusion.table_ref, bf16[4096,1024]{1,0:T(8,128)(2,1)S(1)} %get-tuple-element.39.window_high, bf16[4096,1024]{1,0:T(8,128)(2,1)S(1)} %get-tuple-element.44.window_low, bf16[768,1024]{1,0:T(8,128)(2,1)S(1)} %get-tuple-element.65.weight_ref, ...), custom_call_target="tpu_custom_call", output_to_operand_aliasing={{}: (6, {})} | custom-call | flops 1 | bytes 1 | tf_op jit(solution)/shard_map/residual/pallas_call | solution.py:185
  74.7 1.4 %fusion = f32[512,256]{1,0:T(8,128)} fusion(f32[256,256]{1,0:T(8,128)S(1)} %get-tuple-element.71, f32[256,256]{1,0:T(8,128)S(1)} %fusion.2, f32[256,256]{1,0:T(8,128)S(1)} %fusion.3), kind=kOutput, calls=%fused_computation.2 | convolution fusion | flops 402784256 | bytes 1310720 | tf_op jit(solution)/shard_map/dot_general | solution.py:20
  76.7 2.6 %residual.6.refs_2_ = f32[4096,1024]{1,0:T(8,128)} custom-call(s32[16]{0:T(128)S(1)} %pad_add_fusion.table_ref, bf16[4096,1024]{1,0:T(8,128)(2,1)S(1)} %get-tuple-element.39.window_high, bf16[4096,1024]{1,0:T(8,128)(2,1)S(1)} %get-tuple-element.44.window_low, bf16[768,1024]{1,0:T(8,128)(2,1)S(1)} %get-tuple-element.65.weight_ref, ...), custom_call_target="tpu_custom_call", output_to_operand_aliasing={{}: (5, {})} | custom-call | flops 1 | bytes 1 | tf_op jit(solution)/shard_map/residual/pallas_call | solution.py:185
  79.3 3.6 %residual.7 = f32[4096,1024]{1,0:T(8,128)} custom-call(s32[16]{0:T(128)S(1)} %pad_add_fusion.table_ref, bf16[4096,1024]{1,0:T(8,128)(2,1)S(1)} %get-tuple-element.39.window_high, bf16[4096,1024]{1,0:T(8,128)(2,1)S(1)} %get-tuple-element.44.window_low, bf16[768,1024]{1,0:T(8,128)(2,1)S(1)} %get-tuple-element.65.weight_ref, ...), custom_call_target="tpu_custom_call", output_to_operand_aliasing={{}: (6, {})} | custom-call | flops 1 | bytes 1 | tf_op jit(solution)/shard_map/residual/pallas_call | solution.py:185
  (37 shorter events, 2.6 us)
Async XLA Ops:
  0.6 23.9 %copy-start = (f32[64,1024]{1,0:T(8,128)S(1)}, f32[64,1024]{1,0:T(8,128)}, u32[]{:S(2)}) copy-start(f32[64,1024]{1,0:T(8,128)} %refs_0_.1) | copy-start | bytes 786436
  0.6 11.2 %collective-permute-start = (f32[64,1024]{1,0:T(8,128)}, f32[64,1024]{1,0:T(8,128)S(1)}, u32[]{:S(2)}, u32[]{:S(2)}) collective-permute-start(f32[64,1024]{1,0:T(8,128)} %refs_0_.1), channel_id=1, source_target_pairs={{0,3},{1,0},{2,1},{3,2},{4,7},{5,4},{6,5},{7,6},{8,11},{9,8},{10,9... | collective-permute-start | bytes 786440 | tf_op jit(solution)/shard_map/ppermute | solution.py:358
  11.8 12.4 %collective-permute-start.2 = (f32[64,1024]{1,0:T(8,128)}, f32[64,1024]{1,0:T(8,128)S(1)}, u32[]{:S(2)}, u32[]{:S(2)}) collective-permute-start(f32[64,1024]{1,0:T(8,128)} %refs_0_.1), channel_id=1, source_target_pairs={{0,1},{1,2},{2,3},{3,0},{4,5},{5,6},{6,7},{7,4},{8,9},{9,10},{10,1... | collective-permute-start | bytes 786440 | tf_op jit(solution)/shard_map/ppermute | solution.py:365
  12.0 12.5 %collective-permute-start.1 = (f32[64,1024]{1,0:T(8,128)S(1)}, f32[64,1024]{1,0:T(8,128)S(1)}, u32[]{:S(2)}, u32[]{:S(2)}) collective-permute-start(f32[64,1024]{1,0:T(8,128)S(1)} %collective-permute-done.refs_1_), channel_id=1, source_target_pairs={{0,3},{1,0},{2,1},{3,2},{4,7},{5,4},{6,5},{7,6},{8,11},{9,8},{10,9... | collective-permute-start | bytes 786440 | tf_op jit(solution)/shard_map/ppermute | solution.py:363
  25.7 6.7 %collective-permute-start.3 = (f32[256,256]{1,0:T(8,128)S(1)}, f32[256,256]{1,0:T(8,128)S(1)}, u32[]{:S(2)}, u32[]{:S(2)}) collective-permute-start(f32[256,256]{1,0:T(8,128)S(1)} %get-tuple-element.42), channel_id=1, source_target_pairs={{0,8},{4,20},{8,0},{12,28},{16,24},{20,4},{24,16},{28,12},{1,9},{5... | collective-permute-start | bytes 786440 | tf_op jit(solution)/shard_map/ppermute | solution.py:330
  29.8 4.2 %collective-permute-start.5 = (f32[1024,256]{1,0:T(8,128)S(1)}, f32[1024,256]{1,0:T(8,128)S(1)}, u32[]{:S(2)}, u32[]{:S(2)}) collective-permute-start(f32[1024,256]{1,0:T(8,128)S(1)} %cross.4), channel_id=1, source_target_pairs={{0,4},{4,0},{8,12},{12,8},{16,20},{20,16},{24,28},{28,24},{1,5},{5... | collective-permute-start | bytes 3145736 | tf_op jit(solution)/shard_map/ppermute | solution.py:325
  32.4 9.2 %collective-permute-start.4 = (f32[256,256]{1,0:T(8,128)S(1)}, f32[256,256]{1,0:T(8,128)S(1)}, u32[]{:S(2)}, u32[]{:S(2)}) collective-permute-start(f32[256,256]{1,0:T(8,128)S(1)} %add.53), channel_id=1, source_target_pairs={{0,16},{4,12},{8,24},{12,4},{16,0},{20,28},{24,8},{28,20},{1,17},{... | collective-permute-start | bytes 786440 | tf_op jit(solution)/shard_map/ppermute | solution.py:330
  34.1 13.0 %collective-permute-start.8 = (f32[512,256]{1,0:T(8,128)S(1)}, f32[512,256]{1,0:T(8,128)S(1)}, u32[]{:S(2)}, u32[]{:S(2)}) collective-permute-start(f32[512,256]{1,0:T(8,128)S(1)} %slice_add_fusion.1), channel_id=1, source_target_pairs={{0,8},{4,20},{8,0},{12,28},{16,24},{20,4},{24,16},{28,12},{1,9},{5... | collective-permute-start | bytes 1572872 | tf_op jit(solution)/shard_map/ppermute | solution.py:330
  37.9 2.8 %collective-permute-start.6 = (f32[1024,256]{1,0:T(8,128)S(1)}, f32[1024,256]{1,0:T(8,128)S(1)}, u32[]{:S(2)}, u32[]{:S(2)}) collective-permute-start(f32[1024,256]{1,0:T(8,128)S(1)} %cross.6), channel_id=1, source_target_pairs={{0,4},{4,0},{8,12},{12,8},{16,20},{20,16},{24,28},{28,24},{1,5},{5... | collective-permute-start | bytes 3145736 | tf_op jit(solution)/shard_map/ppermute | solution.py:325
  40.8 9.3 %collective-permute-start.9 = (f32[512,256]{1,0:T(8,128)S(1)}, f32[512,256]{1,0:T(8,128)S(1)}, u32[]{:S(2)}, u32[]{:S(2)}) collective-permute-start(f32[512,256]{1,0:T(8,128)S(1)} %slice_add_fusion), channel_id=1, source_target_pairs={{0,8},{4,20},{8,0},{12,28},{16,24},{20,4},{24,16},{28,12},{1,9},{5... | collective-permute-start | bytes 1572872 | tf_op jit(solution)/shard_map/ppermute | solution.py:330
  41.7 1.6 %collective-permute-start.7 = (f32[256,256]{1,0:T(8,128)S(1)}, f32[256,256]{1,0:T(8,128)S(1)}, u32[]{:S(2)}, u32[]{:S(2)}) collective-permute-start(f32[256,256]{1,0:T(8,128)S(1)} %add.56), channel_id=1, source_target_pairs={{0,4},{4,0},{8,12},{12,8},{16,20},{20,16},{24,28},{28,24},{1,5},{5... | collective-permute-start | bytes 786440 | tf_op jit(solution)/shard_map/ppermute | solution.py:325
  47.1 7.8 %collective-permute-start.10 = (f32[256,256]{1,0:T(8,128)S(1)}, f32[256,256]{1,0:T(8,128)S(1)}, u32[]{:S(2)}, u32[]{:S(2)}) collective-permute-start(f32[256,256]{1,0:T(8,128)S(1)} %slice_add_fusion.8), channel_id=1, source_target_pairs={{0,16},{4,12},{8,24},{12,4},{16,0},{20,28},{24,8},{28,20},{1,17},{... | collective-permute-start | bytes 786440 | tf_op jit(solution)/shard_map/ppermute | solution.py:330
  50.1 6.4 %collective-permute-start.11 = (f32[256,256]{1,0:T(8,128)S(1)}, f32[256,256]{1,0:T(8,128)S(1)}, u32[]{:S(2)}, u32[]{:S(2)}) collective-permute-start(f32[256,256]{1,0:T(8,128)S(1)} %slice_add_fusion.6), channel_id=1, source_target_pairs={{0,16},{4,12},{8,24},{12,4},{16,0},{20,28},{24,8},{28,20},{1,17},{... | collective-permute-start | bytes 786440 | tf_op jit(solution)/shard_map/ppermute | solution.py:330
  55.0 6.7 %collective-permute-start.13 = (f32[256,256]{1,0:T(8,128)S(1)}, f32[256,256]{1,0:T(8,128)S(1)}, u32[]{:S(2)}, u32[]{:S(2)}) collective-permute-start(f32[256,256]{1,0:T(8,128)S(1)} %fusion.3), channel_id=1, source_target_pairs={{0,16},{4,12},{8,24},{12,4},{16,0},{20,28},{24,8},{28,20},{1,17},{... | collective-permute-start | bytes 786440 | tf_op jit(solution)/shard_map/ppermute | solution.py:330
  56.6 7.7 %collective-permute-start.12 = (f32[256,256]{1,0:T(8,128)S(1)}, f32[256,256]{1,0:T(8,128)S(1)}, u32[]{:S(2)}, u32[]{:S(2)}) collective-permute-start(f32[256,256]{1,0:T(8,128)S(1)} %fusion.2), channel_id=1, source_target_pairs={{0,16},{4,12},{8,24},{12,4},{16,0},{20,28},{24,8},{28,20},{1,17},{... | collective-permute-start | bytes 786440 | tf_op jit(solution)/shard_map/ppermute | solution.py:330
  61.8 3.2 %collective-permute-start.17 = (f32[512,256]{1,0:T(8,128)S(1)}, f32[512,256]{1,0:T(8,128)S(1)}, u32[]{:S(2)}, u32[]{:S(2)}) collective-permute-start(f32[512,256]{1,0:T(8,128)S(1)} %pad_maximum_fusion.3.refs_0_), channel_id=1, source_target_pairs={{0,4},{4,0},{8,12},{12,8},{16,20},{20,16},{24,28},{28,24},{1,5},{5... | collective-permute-start | bytes 1572872 | tf_op jit(solution)/shard_map/ppermute | solution.py:325
  61.8 9.2 %collective-permute-start.16 = (f32[512,256]{1,0:T(8,128)S(1)}, f32[512,256]{1,0:T(8,128)S(1)}, u32[]{:S(2)}, u32[]{:S(2)}) collective-permute-start(f32[512,256]{1,0:T(8,128)S(1)} %pad_maximum_fusion.3.refs_0_), channel_id=1, source_target_pairs={{0,8},{4,20},{8,0},{12,28},{16,24},{20,4},{24,16},{28,12},{1,9},{5... | collective-permute-start | bytes 1572872 | tf_op jit(solution)/shard_map/ppermute | solution.py:330
  64.3 6.8 %collective-permute-start.15 = (f32[512,256]{1,0:T(8,128)S(1)}, f32[512,256]{1,0:T(8,128)S(1)}, u32[]{:S(2)}, u32[]{:S(2)}) collective-permute-start(f32[512,256]{1,0:T(8,128)S(1)} %pad_maximum_fusion.1.refs_2_), channel_id=1, source_target_pairs={{0,4},{4,0},{8,12},{12,8},{16,20},{20,16},{24,28},{28,24},{1,5},{5... | collective-permute-start | bytes 1572872 | tf_op jit(solution)/shard_map/ppermute | solution.py:325
  64.4 12.3 %collective-permute-start.14 = (f32[512,256]{1,0:T(8,128)S(1)}, f32[512,256]{1,0:T(8,128)S(1)}, u32[]{:S(2)}, u32[]{:S(2)}) collective-permute-start(f32[512,256]{1,0:T(8,128)S(1)} %pad_maximum_fusion.1.refs_2_), channel_id=1, source_target_pairs={{0,8},{4,20},{8,0},{12,28},{16,24},{20,4},{24,16},{28,12},{1,9},{5... | collective-permute-start | bytes 1572872 | tf_op jit(solution)/shard_map/ppermute | solution.py:330
  71.1 8.2 %collective-permute-start.18 = (f32[512,256]{1,0:T(8,128)S(1)}, f32[512,256]{1,0:T(8,128)S(1)}, u32[]{:S(2)}, u32[]{:S(2)}) collective-permute-start(f32[512,256]{1,0:T(8,128)S(1)} %collective-permute-done.16.refs_1_), channel_id=1, source_target_pairs={{0,4},{4,0},{8,12},{12,8},{16,20},{20,16},{24,28},{28,24},{1,5},{5... | collective-permute-start | bytes 1572872 | tf_op jit(solution)/shard_map/ppermute | solution.py:325
  76.7 2.6 %collective-permute-start.19 = (f32[512,256]{1,0:T(8,128)S(1)}, f32[512,256]{1,0:T(8,128)S(1)}, u32[]{:S(2)}, u32[]{:S(2)}) collective-permute-start(f32[512,256]{1,0:T(8,128)S(1)} %collective-permute-done.14.refs_0_), channel_id=1, source_target_pairs={{0,4},{4,0},{8,12},{12,8},{16,20},{20,16},{24,28},{28,24},{1,5},{5... | collective-permute-start | bytes 1572872 | tf_op jit(solution)/shard_map/ppermute | solution.py:325
